TPU v7x, 32 devices: a whole 2x2x4 slice. The times are simulated.
32 devices in a mesh: row: 4 (over z), col: 8 (over y, x, core).
Axes of the slice: x: 2, y: 2, z: 4, core: 2. Of those that a mesh axis runs over, the one named last changes fastest.
Arguments:
- gradient: bfloat16 [4096, 6144], P('row', 'col'), may hold values from -1.5 to 1.5
- left_stat: float32 [4096, 4096], P('col', 'row'), may hold values from -6 to 6
- left_basis: bfloat16 [4096, 4096], P('col', 'row'), may hold values from -0.09375 to 0.09375
- right_basis: bfloat16 [6144, 6144], P('row', 'col'), may hold values from -0.078125 to 0.078125
- first_moment: float32 [4096, 6144], P('row', 'col'), may hold values from -0.625 to 0.625
- second_moment: float32 [4096, 6144], P('row', 'col'), may hold values from 0.01 to 0.1
Outputs:
- left_next: float32 [4096, 4096], P('col', 'row')
- first_next: float32 [4096, 6144], P('row', 'col')
- second_next: float32 [4096, 6144], P('row', 'col')
- direction: bfloat16 [4096, 6144], P('row', 'col')
All inputs are finite; a program needn't handle non-finite values.
Results may differ from a plain program's by a relative error of at most 0.015.
Values may be sent and summed in bfloat16 or wider, within the bound.
No kernel may reach another device: no remote copies, remote signals or barrier semaphores. Data moves between devices by JAX's collectives and lax.ppermute only.
A program may use at most 128 MiB of HBM per device.

v0:
```python
import jax
import jax.numpy as jnp
from jax import lax
from jax.sharding import PartitionSpec as P


def contract_last(first, second):
    return lax.dot_general(
        first, second, (((1,), (1,)), ((), ())), preferred_element_type=jnp.float32
    )


def contract_first(first, second):
    return lax.dot_general(
        first, second, (((0,), (0,)), ((), ())), preferred_element_type=jnp.float32
    )


def body(gradient, left_stat, left_basis, right_basis, first_moment, second_moment):
    right_cols = lax.all_gather(right_basis, "row", axis=0, tiled=True)
    left_cols = lax.all_gather(left_basis, "col", axis=0, tiled=True)
    subset = right_cols
    half_rotated = jnp.dot(
        lax.all_gather(gradient, "col", axis=1, tiled=True),
        subset,
        preferred_element_type=jnp.float32,
    ).astype(jnp.bfloat16)
    columns = lax.all_gather(gradient, "row", axis=0, tiled=True)
    subset = columns
    product = lax.psum_scatter(
        contract_last(subset, gradient).astype(jnp.bfloat16), "col", scatter_dimension=0, tiled=True
    ).astype(jnp.float32)
    left_next = 0.95 * left_stat + 0.05 * product
    subset = left_cols
    rotated = contract_first(subset, lax.all_gather(half_rotated, "row", axis=0, tiled=True))
    first_next = 0.9 * first_moment + 0.1 * rotated
    second_next = 0.95 * second_moment + 0.05 * rotated * rotated
    scaled_first = first_next / (1.0 - 0.9**10)
    scaled_second = second_next / (1.0 - 0.95**10)
    normalized = (scaled_first / (jnp.sqrt(scaled_second) + 1e-08)).astype(jnp.bfloat16)
    subset = right_cols
    back_t = lax.psum_scatter(
        contract_last(subset, normalized).astype(jnp.bfloat16),
        "col",
        scatter_dimension=0,
        tiled=True,
    )
    subset = left_cols
    direction = lax.psum_scatter(
        contract_last(subset, back_t).astype(jnp.bfloat16), "row", scatter_dimension=0, tiled=True
    )
    return (left_next, first_next, second_next, direction)


def solution(mesh):
    return jax.shard_map(
        body,
        mesh=mesh,
        in_specs=(
            P("row", "col"),
            P("col", "row"),
            P("col", "row"),
            P("row", "col"),
            P("row", "col"),
            P("row", "col"),
        ),
        out_specs=(P("col", "row"), P("row", "col"), P("row", "col"), P("row", "col")),
        check_vma=False,
    )
```

profile of v0, /device:TPU:0, one launch (start us, length us, event | category | flops | bytes accessed | tf_op | source)
XLA Modules:
  0.0 831.1 jit_solution(12397524192618157043)
XLA Ops:
  7.2 0.7 all-gather.10.cloned.1.call-update
  7.9 0.7 all-gather.8.cloned.1.call-update
  8.7 0.7 all-gather.14.cloned.1.call-update
  9.4 169.6 %all-gather.10.cloned.1.call-done = bf16[6144,768]{1,0:T(8,128)(2,1)} async-done(((bf16[1536,768]{1,0:T(8,128)(2,1)}), bf16[6144,768]{1,0:T(8,128)(2,1)}) %all-gather.10.cloned.1.call-update) | async-done | bytes 9437200 | tf_op jit(solution)/shard_map/all_gather | solution.py:20
  179.1 72.0 %all-gather.8.cloned.1.call-done = bf16[1024,6144]{1,0:T(8,128)(2,1)} async-done(((bf16[1024,768]{1,0:T(8,128)(2,1)}), bf16[1024,6144]{1,0:T(8,128)(2,1)}) %all-gather.8.cloned.1.call-update) | async-done | bytes 12582928 | tf_op jit(solution)/shard_map/all_gather | solution.py:24
  251.0 15.6 %convolution_convert_fusion.2 = bf16[1024,768]{1,0:T(8,128)(2,1)} fusion(bf16[1024,6144]{1,0:T(8,128)(2,1)} %all-gather.8.cloned.1.call-done, bf16[6144,768]{1,0:T(8,128)(2,1)} %all-gather.10.cloned.1.call-done), kind=kOutput, calls=%fused_computation.10 | convolution fusion | flops 9664462848 | bytes 23592960 | tf_op jit(solution)/shard_map/dot_general | solution.py:23
  266.7 0.5 all-gather.6.cloned.1.call-update
  267.5 1.0 copy-done
  268.5 2.4 copy.10
  270.9 3.5 copy.11
  274.4 33.0 %all-gather.14.cloned.1.call-done = bf16[4096,1024]{1,0:T(8,128)(2,1)} async-done(((bf16[512,1024]{1,0:T(8,128)(2,1)}), bf16[4096,1024]{1,0:T(8,128)(2,1)}) %all-gather.14.cloned.1.call-update) | async-done | bytes 8388624 | tf_op jit(solution)/shard_map/all_gather | solution.py:21
  307.4 117.4 %all-gather.12.cloned.1.call-done = bf16[4096,768]{1,0:T(8,128)(2,1)} async-done(((bf16[1024,768]{1,0:T(8,128)(2,1)}), bf16[4096,768]{1,0:T(8,128)(2,1)}) %all-gather.12.cloned.1.call-update) | async-done | bytes 6291472 | tf_op jit(solution)/shard_map/all_gather | solution.py:35
  424.7 14.2 %fusion.1 = (f32[1024,768]{0,1:T(8,128)S(1)}, f32[1024,768]{0,1:T(8,128)}) fusion(f32[1024,768]{0,1:T(8,128)} %copy.11, f32[1024,768]{0,1:T(8,128)} %copy.10, bf16[4096,768]{1,0:T(8,128)(2,1)} %all-gather.12.cloned.1.call-done, bf16[4096,1024]{1,0:T(8,128)(2,1)} %all-gather.14.cloned.1.call-done), kind=kOutput, calls=%fused_computation.5 | convolution fusion | flops 6447955968 | bytes 27262976 | tf_op jit(solution)/shard_map/dot_general | solution.py:14
  439.0 18.5 %convert_bitcast_fusion = bf16[6144,1024]{0,1:T(8,128)(2,1)} fusion(bf16[6144,768]{1,0:T(8,128)(2,1)} %all-gather.10.cloned.1.call-done, f32[1024,768]{0,1:T(8,128)S(1)} %get-tuple-element.8, f32[1024,768]{0,1:T(8,128)} %get-tuple-element.9), kind=kOutput, calls=%fused_computation | convolution fusion | flops 9673900032 | bytes 28311552 | tf_op jit(solution)/shard_map/dot_general | solution.py:8
  457.7 82.0 %all-gather.6.cloned.1.call-done = bf16[4096,768]{1,0:T(8,128)(2,1)} async-done(((bf16[1024,768]{1,0:T(8,128)(2,1)}), bf16[4096,768]{1,0:T(8,128)(2,1)}) %all-gather.6.cloned.1.call-update) | async-done | bytes 6291472 | tf_op jit(solution)/shard_map/all_gather | solution.py:28
  539.8 11.9 %convolution_convert_fusion = bf16[4096,1024]{1,0:T(8,128)(2,1)} fusion(bf16[4096,768]{1,0:T(8,128)(2,1)} %all-gather.6.cloned.1.call-done, bf16[1024,768]{1,0:T(8,128)(2,1)} %param.6), kind=kOutput, calls=%fused_computation.1 | convolution fusion | flops 6446645248 | bytes 16252928 | tf_op jit(solution)/shard_map/dot_general | solution.py:8
  551.8 82.0 %reduce-scatter.6.cloned.1.call-done = bf16[768,1024]{0,1:T(8,128)(2,1)} async-done(((bf16[6144,1024]{0,1:T(8,128)(2,1)}), bf16[768,1024]{0,1:T(8,128)(2,1)}) %reduce-scatter.6.cloned.1.call-update) | async-done | bytes 1572880 | tf_op jit(solution)/shard_map/reduce_scatter | solution.py:42
  633.8 11.3 %fusion = bf16[4096,768]{0,1:T(8,128)(2,1)} fusion(bf16[768,1024]{0,1:T(8,128)(2,1)} %reduce-scatter.6.cloned.1.call-done, bf16[4096,1024]{1,0:T(8,128)(2,1)} %all-gather.14.cloned.1.call-done), kind=kOutput, calls=%fused_computation.3 | convolution fusion | flops 6445596672 | bytes 16252928 | tf_op jit(solution)/shard_map/dot_general | solution.py:8
  645.1 63.5 %reduce-scatter.4.cloned.1.call-done = bf16[512,1024]{1,0:T(8,128)(2,1)} async-done(((bf16[4096,1024]{1,0:T(8,128)(2,1)}), bf16[512,1024]{1,0:T(8,128)(2,1)}) %reduce-scatter.4.cloned.1.call-update) | async-done | bytes 1048592 | tf_op jit(solution)/shard_map/reduce_scatter | solution.py:30
  708.5 3.7 multiply_add_fusion
  712.3 3.5 copy.12
  715.8 2.6 copy.13
  718.4 103.3 %reduce-scatter.8.cloned.1.call-done = bf16[1024,768]{0,1:T(8,128)(2,1)} async-done(((bf16[4096,768]{0,1:T(8,128)(2,1)}), bf16[1024,768]{0,1:T(8,128)(2,1)}) %reduce-scatter.8.cloned.1.call-update) | async-done | bytes 1572880 | tf_op jit(solution)/shard_map/reduce_scatter | solution.py:49
  821.7 2.6 copy.14
  (13 shorter events, 0.8 us)
Async XLA Ops:
  7.2 171.9 %all-gather.10.cloned.1.call-start = ((), (), s32[]{:S(2)}) async-start(), calls=%async_computation.6 | async-start | bytes 11796480 | tf_op jit(solution)/shard_map/all_gather | solution.py:20
  7.9 243.2 %all-gather.8.cloned.1.call-start = ((), (), s32[]{:S(2)}) async-start(), calls=%async_computation.5 | async-start | bytes 14155776 | tf_op jit(solution)/shard_map/all_gather | solution.py:24
  8.6 298.7 %all-gather.14.cloned.1.call-start = ((), (), s32[]{:S(2)}) async-start(), calls=%async_computation.8 | async-start | bytes 9437184 | tf_op jit(solution)/shard_map/all_gather | solution.py:21
  9.4 415.4 %all-gather.12.cloned.1.call-start = ((), (), s32[]{:S(2)}) async-start(), calls=%async_computation.7 | async-start | bytes 7864320 | tf_op jit(solution)/shard_map/all_gather | solution.py:35
  266.6 1.9 copy-start
  266.6 273.1 %all-gather.6.cloned.1.call-start = ((), (), s32[]{:S(2)}) async-start(), calls=%async_computation.3 | async-start | bytes 7864320 | tf_op jit(solution)/shard_map/all_gather | solution.py:28
  267.2 366.6 %reduce-scatter.6.cloned.1.call-start = ((), (), s32[]{:S(2)}) async-start(), calls=%async_computation.9 | async-start | bytes 14155776 | tf_op jit(solution)/shard_map/reduce_scatter | solution.py:42
  457.5 251.1 %reduce-scatter.4.cloned.1.call-start = ((), (), s32[]{:S(2)}) async-start(), calls=%async_computation.4 | async-start | bytes 9437184 | tf_op jit(solution)/shard_map/reduce_scatter | solution.py:30
  551.7 270.0 %reduce-scatter.8.cloned.1.call-start = ((), (), s32[]{:S(2)}) async-start(), calls=%async_computation.10 | async-start | bytes 7864320 | tf_op jit(solution)/shard_map/reduce_scatter | solution.py:49
Sparse Core Ops, SparseCore 0:
  9.6 169.4 all-gather.9
  181.0 70.0 all-gather.7
  252.9 54.3 all-gather.13
  309.4 115.3 all-gather.11
  426.2 113.5 all-gather.5
  543.1 90.6 reduce-scatter.5
  637.3 71.2 reduce-scatter.3
  711.0 110.7 reduce-scatter.7
where the time goes:
time: 831 us
  waiting for transfers between devices  726 us (87%)
  matrix products  71.4 us (9%)
  local copies, waits for them, and re-layouts  15.6 us (2%)
  between operations  14.1 us (2%)
    all_gather x1, waiting for transfers between devices, body(): right_cols = lax.all_gather(right_basis, 'row', axis=0, tiled=True)  170 us
    all_gather x1, waiting for transfers between devices, body(): lax.all_gather(half_rotated, 'row', axis=0, tiled=True)  117 us
    reduce_scatter x1, waiting for transfers between devices, body(): lax.psum_scatter(contract_last(subset, back_t).astype(jnp.bfloat16), 'row...  103 us
    reduce_scatter x1, waiting for transfers between devices, body(): lax.psum_scatter(contract_last(subset, normalized).astype(jnp.bfloat16),...  82 us
    all_gather x1, waiting for transfers between devices, body(): columns = lax.all_gather(gradient, 'row', axis=0, tiled=True)  82 us
    all_gather x1, waiting for transfers between devices, body(): lax.all_gather(gradient, 'col', axis=1, tiled=True)  72 us
    reduce_scatter x1, waiting for transfers between devices, body(): lax.psum_scatter(contract_last(subset, gradient).astype(jnp.bfloat16), 'c...  63.5 us
    dot_general x3, matrix products, contract_last(): lax.dot_general(first, second, (((1,), (1,)), ((), ())), preferred_elemen...  41.6 us
  transfers between devices with their start and end apart: 8, of which 8 were waited for; matrix products, arithmetic and copies ran while one was open for 10% of the time, Pallas kernels for 0%

commit v1 on v0

v1 whole, which is shorter than its diff:
```python
import jax
import jax.numpy as jnp
from jax import lax
from jax.sharding import PartitionSpec as P


def contract_last(first, second):
    return lax.dot_general(
        first, second, (((1,), (1,)), ((), ())), preferred_element_type=jnp.float32
    )


def contract_first(first, second):
    return lax.dot_general(
        first, second, (((0,), (0,)), ((), ())), preferred_element_type=jnp.float32
    )


def body(gradient, left_stat, left_basis, right_basis, first_moment, second_moment):
    columns = lax.all_gather(gradient, "row", axis=0, tiled=True)
    left_cols = lax.all_gather(left_basis, "col", axis=0, tiled=True)
    right_cols = lax.all_gather(right_basis, "row", axis=0, tiled=True)
    left_rotated = contract_first(left_cols, columns).astype(jnp.bfloat16)
    left_rotated = lax.all_gather(left_rotated, "col", axis=1, tiled=True)
    product = lax.psum_scatter(
        contract_last(columns, gradient).astype(jnp.bfloat16), "col", scatter_dimension=0, tiled=True
    ).astype(jnp.float32)
    left_next = 0.95 * left_stat + 0.05 * product
    rotated = jnp.dot(left_rotated, right_cols, preferred_element_type=jnp.float32)
    first_next = 0.9 * first_moment + 0.1 * rotated
    second_next = 0.95 * second_moment + 0.05 * rotated * rotated
    scaled_first = first_next / (1.0 - 0.9**10)
    scaled_second = second_next / (1.0 - 0.95**10)
    normalized = (scaled_first / (jnp.sqrt(scaled_second) + 1e-08)).astype(jnp.bfloat16)
    back = lax.psum_scatter(
        jnp.dot(left_cols, normalized, preferred_element_type=jnp.float32).astype(jnp.bfloat16),
        "row",
        scatter_dimension=0,
        tiled=True,
    )
    direction = lax.psum_scatter(
        contract_last(back, right_cols).astype(jnp.bfloat16), "col", scatter_dimension=1, tiled=True
    )
    return (left_next, first_next, second_next, direction)


def solution(mesh):
    return jax.shard_map(
        body,
        mesh=mesh,
        in_specs=(
            P("row", "col"),
            P("col", "row"),
            P("col", "row"),
            P("row", "col"),
            P("row", "col"),
            P("row", "col"),
        ),
        out_specs=(P("col", "row"), P("row", "col"), P("row", "col"), P("row", "col")),
        check_vma=False,
    )
```

time: 831 us -> 745 us (0.90)
  waiting for transfers between devices: 726 us -> 654 us
  local copies, waits for them, and re-layouts: 15.6 us -> 3.85 us
    all_gather x2 -> x1, waiting for transfers between devices: 189 us -> 72.4 us  [body(): left_rotated = lax.all_gather(left_rotated, 'col', axis=1, tiled=True)]
    all_gather x1, waiting for transfers between devices: 82 us -> 118 us  [body(): columns = lax.all_gather(gradient, 'row', axis=0, tiled=True)]
    all_gather x1, waiting for transfers between devices: 33 us -> 54.5 us  [body(): left_cols = lax.all_gather(left_basis, 'col', axis=0, tiled=True)]
    dot_general x1 -> x2, matrix products: 15.6 us -> 29.4 us  [the longest x1 16.2 us: body(): jnp.dot(left_rotated, right_cols, preferred_element_type=jnp.float32)]
    dot_general x3 -> x2, matrix products: 41.6 us -> 28.3 us  [contract_last(): lax.dot_general(first, second, (((1,), (1,)), ((), ())), preferred_elemen...]
    all_gather x1, waiting for transfers between devices: 170 us -> 156 us  [body(): right_cols = lax.all_gather(right_basis, 'row', axis=0, tiled=True)]
    unnamed x7 -> x10, local copies, waits for them, and re-layouts: 15.6 us -> 3.85 us
  transfers between devices with their start and end apart: 8 -> 7, of which waited for: 8 -> 7; matrix products, arithmetic and copies ran while one was open for 10% -> 6% of each run, Pallas kernels for 0% -> 0%
where the time goes in v1:
time: 745 us
  waiting for transfers between devices  654 us (88%)
  matrix products  69.6 us (9%)
  between operations  14.2 us (2%)
    all_gather x1, waiting for transfers between devices, body(): right_cols = lax.all_gather(right_basis, 'row', axis=0, tiled=True)  156 us
    all_gather x1, waiting for transfers between devices, body(): columns = lax.all_gather(gradient, 'row', axis=0, tiled=True)  118 us
    reduce_scatter x1, waiting for transfers between devices, body(): lax.psum_scatter(jnp.dot(left_cols, normalized, preferred_element_type=jn...  97.6 us
    reduce_scatter x1, waiting for transfers between devices, body(): lax.psum_scatter(contract_last(back, right_cols).astype(jnp.bfloat16), 'c...  94 us
    all_gather x1, waiting for transfers between devices, body(): left_rotated = lax.all_gather(left_rotated, 'col', axis=1, tiled=True)  72.4 us
    reduce_scatter x1, waiting for transfers between devices, body(): lax.psum_scatter(contract_last(columns, gradient).astype(jnp.bfloat16), '...  58.7 us
    all_gather x1, waiting for transfers between devices, body(): left_cols = lax.all_gather(left_basis, 'col', axis=0, tiled=True)  54.5 us
    dot_general x2, matrix products, contract_last(): lax.dot_general(first, second, (((1,), (1,)), ((), ())), preferred_elemen...  28.3 us
  transfers between devices with their start and end apart: 7, of which 7 were waited for; matrix products, arithmetic and copies ran while one was open for 6% of the time, Pallas kernels for 0%

profile of v1, /device:TPU:0, one launch (start us, length us, event | category | flops | bytes accessed | tf_op | source)
XLA Modules:
  0.0 744.9 jit_solution(10489289543753005069)
XLA Ops:
  7.2 0.7 all-gather.5.cloned.1.call-update
  7.9 0.0 all-gather.7.cloned.1.call-start
  7.9 0.7 all-gather.7.cloned.1.call-update
  8.7 0.7 all-gather.11.cloned.1.call-update
  9.4 0.0 all-gather.9.cloned.1.call-start
  9.4 118.2 %all-gather.5.cloned.1.call-done = bf16[4096,768]{1,0:T(8,128)(2,1)} async-done(((bf16[1024,768]{1,0:T(8,128)(2,1)}), bf16[4096,768]{1,0:T(8,128)(2,1)}) %all-gather.5.cloned.1.call-update) | async-done | bytes 6291472 | tf_op jit(solution)/shard_map/all_gather | solution.py:20
  127.7 54.5 %all-gather.7.cloned.1.call-done = bf16[4096,1024]{1,0:T(8,128)(2,1)} async-done(((bf16[512,1024]{1,0:T(8,128)(2,1)}), bf16[4096,1024]{1,0:T(8,128)(2,1)}) %all-gather.7.cloned.1.call-update) | async-done | bytes 8388624 | tf_op jit(solution)/shard_map/all_gather | solution.py:21
  182.2 11.9 %convolution_convert_fusion.3 = bf16[1024,768]{1,0:T(8,128)(2,1)} fusion(bf16[4096,1024]{1,0:T(8,128)(2,1)} %all-gather.7.cloned.1.call-done, bf16[4096,768]{1,0:T(8,128)(2,1)} %all-gather.5.cloned.1.call-done), kind=kOutput, calls=%fused_computation.9 | convolution fusion | flops 6443237376 | bytes 16252928 | tf_op jit(solution)/shard_map/dot_general | solution.py:14
  194.1 0.0 reduce-scatter.6.cloned.1.call-start
  194.2 156.4 %all-gather.11.cloned.1.call-done = bf16[6144,768]{1,0:T(8,128)(2,1)} async-done(((bf16[1536,768]{1,0:T(8,128)(2,1)}), bf16[6144,768]{1,0:T(8,128)(2,1)}) %all-gather.11.cloned.1.call-update) | async-done | bytes 9437200 | tf_op jit(solution)/shard_map/all_gather | solution.py:22
  350.6 72.4 %all-gather.9.cloned.1.call-done = bf16[1024,6144]{1,0:T(8,128)(2,1)} async-done(((bf16[1024,768]{1,0:T(8,128)(2,1)}), bf16[1024,6144]{1,0:T(8,128)(2,1)}) %all-gather.9.cloned.1.call-update) | async-done | bytes 12582928 | tf_op jit(solution)/shard_map/all_gather | solution.py:24
  423.0 16.2 %fusion.1 = (f32[1024,768]{1,0:T(8,128)S(1)}, f32[1024,768]{1,0:T(8,128)S(1)}) fusion(f32[1024,768]{1,0:T(8,128)S(1)} %copy-done.2, f32[1024,768]{1,0:T(8,128)} %param.10, bf16[1024,6144]{1,0:T(8,128)(2,1)} %all-gather.9.cloned.1.call-done, bf16[6144,768]{1,0:T(8,128)(2,1)} %all-gather.11.cloned.1.call-done), kind=kOutput, calls=%fused_computation.5 | convolution fusion | flops 9669181440 | bytes 34603008 | tf_op jit(solution)/shard_map/dot_general | solution.py:29
  439.2 1.6 copy-done.3
  440.8 1.0 copy-done.4
  441.9 13.2 %fusion = bf16[4096,768]{0,1:T(8,128)(2,1)} fusion(bf16[4096,1024]{1,0:T(8,128)(2,1)} %all-gather.7.cloned.1.call-done, f32[1024,768]{1,0:T(8,128)S(1)} %get-tuple-element.4, f32[1024,768]{1,0:T(8,128)S(1)} %get-tuple-element.5), kind=kOutput, calls=%fused_computation.3 | convolution fusion | flops 6449528832 | bytes 20971520 | tf_op jit(solution)/shard_map/dot_general | solution.py:36
  455.1 0.2 reduce-scatter.4.cloned.1.call-start
  455.4 1.2 copy-done.1
  456.5 11.8 %convolution_convert_fusion.1 = bf16[4096,1024]{1,0:T(8,128)(2,1)} fusion(bf16[4096,768]{1,0:T(8,128)(2,1)} %all-gather.5.cloned.1.call-done, bf16[1024,768]{1,0:T(8,128)(2,1)S(1)} %copy-done.1), kind=kOutput, calls=%fused_computation.1 | convolution fusion | flops 6446645248 | bytes 16252928 | tf_op jit(solution)/shard_map/dot_general | solution.py:8
  468.4 0.0 reduce-scatter.8.cloned.1.call-start
  468.4 97.6 %reduce-scatter.6.cloned.1.call-done = bf16[1024,768]{0,1:T(8,128)(2,1)} async-done(((bf16[4096,768]{0,1:T(8,128)(2,1)}), bf16[1024,768]{0,1:T(8,128)(2,1)}) %reduce-scatter.6.cloned.1.call-update) | async-done | bytes 1572880 | tf_op jit(solution)/shard_map/reduce_scatter | solution.py:35
  566.0 16.4 %convolution_convert_fusion = bf16[1024,6144]{1,0:T(8,128)(2,1)} fusion(bf16[1024,768]{0,1:T(8,128)(2,1)} %reduce-scatter.6.cloned.1.call-done, bf16[6144,768]{1,0:T(8,128)(2,1)} %all-gather.11.cloned.1.call-done), kind=kOutput, calls=%fused_computation | convolution fusion | flops 9669967872 | bytes 23592960 | tf_op jit(solution)/shard_map/dot_general | solution.py:8
  582.5 58.7 %reduce-scatter.4.cloned.1.call-done = bf16[512,1024]{1,0:T(8,128)(2,1)} async-done(((bf16[4096,1024]{1,0:T(8,128)(2,1)}), bf16[512,1024]{1,0:T(8,128)(2,1)}) %reduce-scatter.4.cloned.1.call-update) | async-done | bytes 1048592 | tf_op jit(solution)/shard_map/reduce_scatter | solution.py:25
  641.2 2.9 multiply_add_fusion.1
  644.1 94.0 %reduce-scatter.8.cloned.1.call-done = bf16[1024,768]{1,0:T(8,128)(2,1)} async-done(((bf16[1024,6144]{1,0:T(8,128)(2,1)}), bf16[1024,768]{1,0:T(8,128)(2,1)}) %reduce-scatter.8.cloned.1.call-update) | async-done | bytes 1572880 | tf_op jit(solution)/shard_map/reduce_scatter | solution.py:41
  (13 shorter events, 0.2 us)
Async XLA Ops:
  7.2 120.5 %all-gather.5.cloned.1.call-start = ((), (), s32[]{:S(2)}) async-start(), calls=%async_computation.3 | async-start | bytes 7864320 | tf_op jit(solution)/shard_map/all_gather | solution.py:20
  7.9 174.3 %all-gather.7.cloned.1.call-start = ((), (), s32[]{:S(2)}) async-start(), calls=%async_computation.5 | async-start | bytes 9437184 | tf_op jit(solution)/shard_map/all_gather | solution.py:21
  8.6 341.9 %all-gather.11.cloned.1.call-start = ((), (), s32[]{:S(2)}) async-start(), calls=%async_computation.7 | async-start | bytes 11796480 | tf_op jit(solution)/shard_map/all_gather | solution.py:22
  9.4 413.6 %copy-start.2 = (f32[1024,768]{1,0:T(8,128)S(1)}, f32[1024,768]{1,0:T(8,128)}, u32[]{:S(2)}) copy-start(f32[1024,768]{1,0:T(8,128)} %param.11) | copy-start | bytes 9437188
  9.4 413.6 %all-gather.9.cloned.1.call-start = ((), (), s32[]{:S(2)}) async-start(), calls=%async_computation.6 | async-start | bytes 14155776 | tf_op jit(solution)/shard_map/all_gather | solution.py:24
  194.1 371.9 %reduce-scatter.6.cloned.1.call-start = ((), (), s32[]{:S(2)}) async-start(), calls=%async_computation.8 | async-start | bytes 7864320 | tf_op jit(solution)/shard_map/reduce_scatter | solution.py:35
  439.2 1.7 copy-start.3
  439.2 2.7 copy-start.4
  455.1 1.4 copy-start.1
  455.1 186.1 %reduce-scatter.4.cloned.1.call-start = ((), (), s32[]{:S(2)}) async-start(), calls=%async_computation.4 | async-start | bytes 9437184 | tf_op jit(solution)/shard_map/reduce_scatter | solution.py:25
  468.4 269.7 %reduce-scatter.8.cloned.1.call-start = ((), (), s32[]{:S(2)}) async-start(), calls=%async_computation.9 | async-start | bytes 14155776 | tf_op jit(solution)/shard_map/reduce_scatter | solution.py:41
  582.5 58.7 %copy-start = (f32[512,1024]{1,0:T(8,128)S(1)}, f32[512,1024]{1,0:T(8,128)}, u32[]{:S(2)}) copy-start(f32[512,1024]{1,0:T(8,128)} %param.7) | copy-start | bytes 6291460
Sparse Core Ops, SparseCore 0:
  9.6 118.0 all-gather.4
  129.5 52.6 all-gather.6
  183.8 166.7 all-gather.10
  352.9 70.0 all-gather.8
  455.2 110.7 reduce-scatter.5
  569.3 71.7 reduce-scatter.3
  645.7 92.3 reduce-scatter.7

commit v2 on v1

v2 whole, which is shorter than its diff:
```python
import jax
import jax.numpy as jnp
from jax import lax
from jax.sharding import PartitionSpec as P


def contract_last(first, second):
    return lax.dot_general(
        first, second, (((1,), (1,)), ((), ())), preferred_element_type=jnp.float32
    )


def contract_first(first, second):
    return lax.dot_general(
        first, second, (((0,), (0,)), ((), ())), preferred_element_type=jnp.float32
    )


def exchange(x, axis, target):
    n = lax.axis_size(axis)
    return lax.ppermute(x, axis, [(j, target(j)) for j in range(n)])


def inner_of_four(axis):
    i = lax.axis_index(axis)
    return (i == 1) | (i == 2)


def relay_target(j):
    return (2, 0, 3, 1)[j]


def gather_rows(x, axis):
    n = lax.axis_size(axis)
    i = lax.axis_index(axis)
    if n == 4:
        mirror = exchange(x, axis, lambda j: j ^ 3)
        near = exchange(x, axis, lambda j: j ^ 1)
        relay = exchange(jnp.where(inner_of_four(axis), mirror, x), axis, relay_target)
        pieces = [(i, x), (i ^ 1, near), (i ^ 3, mirror), (i ^ 2, relay)]
    else:
        pieces = [(i, x)]
        for s in range(1, n):
            pieces.append(((i + s) % n, exchange(x, axis, lambda j: (j - s) % n)))
    rows, cols = x.shape
    whole = jnp.zeros((n * rows, cols), x.dtype)
    for index, piece in pieces:
        whole = lax.dynamic_update_slice(whole, piece, (index * rows, 0))
    return whole


def scatter_rows(x, axis):
    n = lax.axis_size(axis)
    i = lax.axis_index(axis)
    rows = x.shape[0] // n

    def part(index):
        return lax.dynamic_slice_in_dim(x, index * rows, rows, 0)

    total = part(i).astype(jnp.float32)
    if n == 4:
        inner = inner_of_four(axis)
        relay = exchange(part(i ^ 2), axis, lambda j: (1, 3, 0, 2)[j])
        near = exchange(part(i ^ 1), axis, lambda j: j ^ 1)
        mirror = part(i ^ 3).astype(jnp.float32) + jnp.where(inner, relay, 0).astype(jnp.float32)
        mirror = exchange(mirror.astype(x.dtype), axis, lambda j: j ^ 3)
        total = total + near.astype(jnp.float32) + mirror.astype(jnp.float32)
        total = total + jnp.where(inner, 0, relay).astype(jnp.float32)
    else:
        for s in range(1, n):
            total = total + exchange(part((i - s) % n), axis, lambda j: (j - s) % n).astype(jnp.float32)
    return total.astype(x.dtype)


def body(gradient, left_stat, left_basis, right_basis, first_moment, second_moment):
    left_cols = lax.all_gather(left_basis, "col", axis=0, tiled=True)
    columns = gather_rows(gradient, "row")
    left_rotated = contract_first(left_cols, columns).astype(jnp.bfloat16)
    left_rotated = lax.all_gather(left_rotated, "col", axis=1, tiled=True)
    product = lax.psum_scatter(
        contract_last(columns, gradient).astype(jnp.bfloat16), "col", scatter_dimension=0, tiled=True
    ).astype(jnp.float32)
    left_next = 0.95 * left_stat + 0.05 * product

    width = gradient.shape[1]
    parts = 3 if width % 384 == 0 else 1
    step = width // parts
    first_out, second_out, right_cols, turned = [], [], [], []
    for p in range(parts):
        cut = slice(p * step, (p + 1) * step)
        right_part = gather_rows(right_basis[:, cut], "row")
        rotated = jnp.dot(left_rotated, right_part, preferred_element_type=jnp.float32)
        first_next = 0.9 * first_moment[:, cut] + 0.1 * rotated
        second_next = 0.95 * second_moment[:, cut] + 0.05 * rotated * rotated
        scaled_first = first_next / (1.0 - 0.9**10)
        scaled_second = second_next / (1.0 - 0.95**10)
        normalized = (scaled_first / (jnp.sqrt(scaled_second) + 1e-08)).astype(jnp.bfloat16)
        back = jnp.dot(left_cols, normalized, preferred_element_type=jnp.float32).astype(jnp.bfloat16)
        turned.append(scatter_rows(back, "row"))
        first_out.append(first_next)
        second_out.append(second_next)
        right_cols.append(right_part)
    direction = lax.psum_scatter(
        contract_last(jnp.concatenate(turned, axis=1), jnp.concatenate(right_cols, axis=1)).astype(jnp.bfloat16),
        "col",
        scatter_dimension=1,
        tiled=True,
    )
    return (left_next, jnp.concatenate(first_out, axis=1), jnp.concatenate(second_out, axis=1), direction)


def solution(mesh):
    return jax.shard_map(
        body,
        mesh=mesh,
        in_specs=(
            P("row", "col"),
            P("col", "row"),
            P("col", "row"),
            P("row", "col"),
            P("row", "col"),
            P("row", "col"),
        ),
        out_specs=(P("col", "row"), P("row", "col"), P("row", "col"), P("row", "col")),
        check_vma=False,
    )
```

time: 745 us -> 537 us (0.72)
  waiting for transfers between devices: 654 us -> 275 us
  starting transfers between devices: 0.46 us -> 104 us
  local copies, waits for them, and re-layouts: 3.85 us -> 53.7 us
  other arithmetic: 2.91 us -> 15.8 us
    all_gather x2 -> x0, waiting for transfers between devices: 275 us -> none  [the longest x1 156 us: body(): right_cols = lax.all_gather(right_basis, 'row', axis=0, tiled=True)]
    ppermute x0 -> x21, waiting for transfers between devices: none -> 197 us  [exchange(): return lax.ppermute(x, axis, [(j, target(j)) for j in range(n)])]
    reduce_scatter x2 -> x1, waiting for transfers between devices: 192 us -> 76.4 us  [body(): lax.psum_scatter(contract_last(jnp.concatenate(turned, axis=1), jnp.conca...]
    ppermute x0 -> x21, starting transfers between devices: none -> 104 us  [exchange(): return lax.ppermute(x, axis, [(j, target(j)) for j in range(n)])]
    all_gather x1, waiting for transfers between devices: 72.4 us -> 0.01 us  [body(): left_rotated = lax.all_gather(left_rotated, 'col', axis=1, tiled=True)]
    reduce_scatter x1, waiting for transfers between devices: 58.7 us -> 0.02 us  [body(): lax.psum_scatter(contract_last(columns, gradient).astype(jnp.bfloat16), '...]
    all_gather x1, waiting for transfers between devices: 54.5 us -> 0.01 us  [body(): left_cols = lax.all_gather(left_basis, 'col', axis=0, tiled=True)]
    unnamed x10 -> x62, local copies, waits for them, and re-layouts: 3.85 us -> 22.1 us
  transfers between devices with their start and end apart: 7 -> 25, of which waited for: 7 -> 14; matrix products, arithmetic and copies ran while one was open for 6% -> 24% of each run, Pallas kernels for 0% -> 0%
where the time goes in v2:
time: 537 us; the launch traced here: 536 us
  waiting for transfers between devices  275 us (51%)
  starting transfers between devices  104 us (19%)
  matrix products  74.4 us (14%)
  local copies, waits for them, and re-layouts  53.7 us (10%)
  other arithmetic  15.8 us (3%)
  between operations  14.1 us (3%)
    ppermute x21, waiting for transfers between devices, exchange(): return lax.ppermute(x, axis, [(j, target(j)) for j in range(n)])  197 us
    ppermute x21, starting transfers between devices, exchange(): return lax.ppermute(x, axis, [(j, target(j)) for j in range(n)])  104 us
    reduce_scatter x1, waiting for transfers between devices, body(): lax.psum_scatter(contract_last(jnp.concatenate(turned, axis=1), jnp.conca...  76.4 us
    dot_general x2, matrix products, contract_last(): lax.dot_general(first, second, (((1,), (1,)), ((), ())), preferred_elemen...  27.1 us
    dot_general x3, matrix products, body(): jnp.dot(left_rotated, right_part, preferred_element_type=jnp.float32)  23 us
    unnamed x62, local copies, waits for them, and re-layouts  22.1 us
    dynamic_update_slice x11, local copies, waits for them, and re-layouts, gather_rows(): whole = lax.dynamic_update_slice(whole, piece, (index * rows, 0))  16.2 us
    dot_general x3, matrix products, body(): jnp.dot(left_cols, normalized, preferred_element_type=jnp.float32)  12.2 us
  transfers between devices with their start and end apart: 25, of which 14 were waited for; matrix products, arithmetic and copies ran while one was open for 24% of the time, Pallas kernels for 0%

profile of v2, /device:TPU:0, one launch (start us, length us, event | category | flops | bytes accessed | tf_op | source)
XLA Modules:
  0.0 536.4 jit_solution(8477651173412104410)
XLA Ops:
  13.1 35.5 %collective-permute-done.1 = bf16[1024,768]{1,0:T(8,128)(2,1)S(1)} collective-permute-done((bf16[1024,768]{1,0:T(8,128)(2,1)}, bf16[1024,768]{1,0:T(8,128)(2,1)S(1)}, u32[]{:S(2)}, u32[]{:S(2)}) %collective-permute-start.1) | collective-permute-done | bytes 1572896 | tf_op jit(solution)/shard_map/ppermute | solution.py:21
  53.8 33.5 %collective-permute-start.2 = (bf16[1024,768]{1,0:T(8,128)(2,1)}, bf16[1024,768]{1,0:T(8,128)(2,1)}, u32[]{:S(2)}, u32[]{:S(2)}) collective-permute-start(bf16[1024,768]{1,0:T(8,128)(2,1)} %get-tuple-element.29), channel_id=1, source_target_pairs={{0,16},{8,0},{16,24},{24,8},{1,17},{9,1},{17,25},{25,9},{2,18},{10... | collective-permute-start | bytes 4718600 | tf_op jit(solution)/shard_map/ppermute | solution.py:21
  89.8 30.6 %collective-permute-done.2 = bf16[1024,768]{1,0:T(8,128)(2,1)} collective-permute-done((bf16[1024,768]{1,0:T(8,128)(2,1)}, bf16[1024,768]{1,0:T(8,128)(2,1)}, u32[]{:S(2)}, u32[]{:S(2)}) %collective-permute-start.2) | collective-permute-done | bytes 1572896 | tf_op jit(solution)/shard_map/ppermute | solution.py:21
  123.0 12.1 %fusion.10 = bf16[1024,768]{0,1:T(8,128)(2,1)} fusion(bf16[4096,768]{1,0:T(8,128)(2,1)} %constant_dynamic-update-slice_fusion.12, bf16[4096,1024]{1,0:T(8,128)(2,1)} %all-gather.3.cloned.1.call-done), kind=kOutput, calls=%fused_computation.23 | convolution fusion | flops 6443237376 | bytes 16252928 | tf_op jit(solution)/shard_map/dot_general | solution.py:14
  144.6 16.9 %collective-permute-done.4 = bf16[1536,256]{1,0:T(8,128)(2,1)S(1)} collective-permute-done((bf16[1536,256]{1,0:T(8,128)(2,1)}, bf16[1536,256]{1,0:T(8,128)(2,1)S(1)}, u32[]{:S(2)}, u32[]{:S(2)}) %collective-permute-start.4) | collective-permute-done | bytes 786464 | tf_op jit(solution)/shard_map/ppermute | solution.py:21
  165.2 14.8 %collective-permute-start.6 = (bf16[1536,256]{1,0:T(8,128)(2,1)}, bf16[1536,256]{1,0:T(8,128)(2,1)}, u32[]{:S(2)}, u32[]{:S(2)}) collective-permute-start(bf16[1536,256]{1,0:T(8,128)(2,1)} %get-tuple-element.17), channel_id=1, source_target_pairs={{0,8},{8,0},{16,24},{24,16},{1,9},{9,1},{17,25},{25,17},{2,10},{10... | collective-permute-start | bytes 2359304 | tf_op jit(solution)/shard_map/ppermute | solution.py:21
  183.9 11.8 %convolution_convert_fusion.1 = bf16[4096,1024]{1,0:T(8,128)(2,1)} fusion(bf16[4096,768]{1,0:T(8,128)(2,1)} %constant_dynamic-update-slice_fusion.12, bf16[1024,768]{1,0:T(8,128)(2,1)S(1)} %copy-done.7), kind=kOutput, calls=%fused_computation.6 | convolution fusion | flops 6446645248 | bytes 16252928 | tf_op jit(solution)/shard_map/dot_general | solution.py:8
  219.3 15.3 %collective-permute-done.10 = bf16[1536,256]{1,0:T(8,128)(2,1)} collective-permute-done((bf16[1536,256]{1,0:T(8,128)(2,1)}, bf16[1536,256]{1,0:T(8,128)(2,1)}, u32[]{:S(2)}, u32[]{:S(2)}) %collective-permute-start.10) | collective-permute-done | bytes 786464 | tf_op jit(solution)/shard_map/ppermute | solution.py:21
  239.5 17.5 %collective-permute-start.8 = (bf16[1536,256]{1,0:T(8,128)(2,1)S(1)}, bf16[1536,256]{1,0:T(8,128)(2,1)S(1)}, u32[]{:S(2)}, u32[]{:S(2)}) collective-permute-start(bf16[1536,256]{1,0:T(8,128)(2,1)S(1)} %get-tuple-element.20), channel_id=1, source_target_pairs={{0,16},{8,0},{16,24},{24,8},{1,17},{9,1},{17,25},{25,9},{2,18},{10... | collective-permute-start | bytes 2359304 | tf_op jit(solution)/shard_map/ppermute | solution.py:21
  261.1 6.4 %collective-permute-done.5 = bf16[1536,256]{1,0:T(8,128)(2,1)S(1)} collective-permute-done((bf16[1536,256]{1,0:T(8,128)(2,1)}, bf16[1536,256]{1,0:T(8,128)(2,1)S(1)}, u32[]{:S(2)}, u32[]{:S(2)}) %collective-permute-start.5) | collective-permute-done | bytes 786464 | tf_op jit(solution)/shard_map/ppermute | solution.py:21
  268.5 15.9 %collective-permute-done.8 = bf16[1536,256]{1,0:T(8,128)(2,1)S(1)} collective-permute-done((bf16[1536,256]{1,0:T(8,128)(2,1)S(1)}, bf16[1536,256]{1,0:T(8,128)(2,1)S(1)}, u32[]{:S(2)}, u32[]{:S(2)}) %collective-permute-start.8) | collective-permute-done | bytes 786464 | tf_op jit(solution)/shard_map/ppermute | solution.py:21
  285.3 15.8 %collective-permute-done.11 = bf16[1536,256]{1,0:T(8,128)(2,1)S(1)} collective-permute-done((bf16[1536,256]{1,0:T(8,128)(2,1)S(1)}, bf16[1536,256]{1,0:T(8,128)(2,1)S(1)}, u32[]{:S(2)}, u32[]{:S(2)}) %collective-permute-start.11) | collective-permute-done | bytes 786464 | tf_op jit(solution)/shard_map/ppermute | solution.py:21
  302.1 7.6 %fusion.12 = (f32[1024,256]{0,1:T(8,128)S(1)}, f32[1024,256]{0,1:T(8,128)S(1)}) fusion(f32[1024,256]{0,1:T(8,128)S(1)} %copy-done.24, f32[1024,256]{0,1:T(8,128)S(1)} %copy-done.23, bf16[1024,6144]{0,1:T(8,128)(2,1)} %all-gather.5.cloned.1.call-done, bf16[6144,256]{1,0:T(8,128)(2,1)} %constant_dynamic-update-slice_fusion.4), kind=kOutput, calls=%fused_computation.25 | convolution fusion | flops 3223060480 | bytes 19922944 | tf_op jit(solution)/shard_map/dot_general | solution.py:92
  309.7 6.8 %convolution_convert_fusion.3 = bf16[256,4096]{1,0:T(8,128)(2,1)S(1)} fusion(bf16[4096,1024]{1,0:T(8,128)(2,1)} %all-gather.3.cloned.1.call-done, f32[1024,256]{0,1:T(8,128)S(1)} %get-tuple-element.33, f32[1024,256]{0,1:T(8,128)S(1)} %get-tuple-element.34), kind=kOutput, calls=%fused_computation.8 | convolution fusion | flops 2149842944 | bytes 12582912 | tf_op jit(solution)/shard_map/dot_general | solution.py:98
  317.3 7.9 %fusion.11 = (f32[1024,256]{0,1:T(8,128)S(1)}, f32[1024,256]{0,1:T(8,128)S(1)}) fusion(f32[1024,256]{0,1:T(8,128)S(1)} %copy-done.22, f32[1024,256]{0,1:T(8,128)S(1)} %copy-done.21, bf16[1024,6144]{0,1:T(8,128)(2,1)} %all-gather.5.cloned.1.call-done, bf16[6144,256]{1,0:T(8,128)(2,1)} %constant_dynamic-update-slice_fusion.8), kind=kOutput, calls=%fused_computation.24 | convolution fusion | flops 3223060480 | bytes 19922944 | tf_op jit(solution)/shard_map/dot_general | solution.py:92
  330.4 7.6 %fusion.13 = (f32[1024,256]{0,1:T(8,128)S(1)}, f32[1024,256]{0,1:T(8,128)S(1)}) fusion(f32[1024,256]{0,1:T(8,128)S(1)} %copy-done.20, f32[1024,256]{0,1:T(8,128)S(1)} %copy-done.19, bf16[1024,6144]{0,1:T(8,128)(2,1)} %all-gather.5.cloned.1.call-done, bf16[6144,256]{1,0:T(8,128)(2,1)} %constant_dynamic-update-slice_fusion), kind=kOutput, calls=%fused_computation.26 | convolution fusion | flops 3223060480 | bytes 19922944 | tf_op jit(solution)/shard_map/dot_general | solution.py:92
  347.8 8.9 %collective-permute-done.19 = bf16[1024,256]{0,1:T(8,128)(2,1)S(1)} collective-permute-done((bf16[1024,256]{0,1:T(8,128)(2,1)S(1)}, bf16[1024,256]{0,1:T(8,128)(2,1)S(1)}, u32[]{:S(2)}, u32[]{:S(2)}) %collective-permute-start.19) | collective-permute-done | bytes 524320 | tf_op jit(solution)/shard_map/ppermute | solution.py:21
  358.5 8.9 %collective-permute-done.15 = bf16[1024,256]{0,1:T(8,128)(2,1)S(1)} collective-permute-done((bf16[1024,256]{0,1:T(8,128)(2,1)S(1)}, bf16[1024,256]{0,1:T(8,128)(2,1)S(1)}, u32[]{:S(2)}, u32[]{:S(2)}) %collective-permute-start.15) | collective-permute-done | bytes 524320 | tf_op jit(solution)/shard_map/ppermute | solution.py:21
  367.3 11.0 %collective-permute-start.20 = (bf16[1024,256]{0,1:T(8,128)(2,1)S(1)}, bf16[1024,256]{0,1:T(8,128)(2,1)S(1)}, u32[]{:S(2)}, u32[]{:S(2)}) collective-permute-start(bf16[1024,256]{0,1:T(8,128)(2,1)S(1)} %fusion.14), channel_id=1, source_target_pairs={{0,24},{8,16},{16,8},{24,0},{1,25},{9,17},{17,9},{25,1},{2,26},{10... | collective-permute-start | bytes 1572872 | tf_op jit(solution)/shard_map/ppermute | solution.py:21
  378.9 9.6 %collective-permute-done.12 = bf16[1024,256]{0,1:T(8,128)(2,1)S(1)} collective-permute-done((bf16[1024,256]{0,1:T(8,128)(2,1)S(1)}, bf16[1024,256]{0,1:T(8,128)(2,1)S(1)}, u32[]{:S(2)}, u32[]{:S(2)}) %collective-permute-start.12) | collective-permute-done | bytes 524320 | tf_op jit(solution)/shard_map/ppermute | solution.py:21
  388.5 23.8 %collective-permute-done.14 = bf16[1024,256]{0,1:T(8,128)(2,1)S(1)} collective-permute-done((bf16[1024,256]{0,1:T(8,128)(2,1)S(1)}, bf16[1024,256]{0,1:T(8,128)(2,1)S(1)}, u32[]{:S(2)}, u32[]{:S(2)}) %collective-permute-start.14) | collective-permute-done | bytes 524320 | tf_op jit(solution)/shard_map/ppermute | solution.py:21
  412.6 9.6 %collective-permute-done.20 = bf16[1024,256]{0,1:T(8,128)(2,1)S(1)} collective-permute-done((bf16[1024,256]{0,1:T(8,128)(2,1)S(1)}, bf16[1024,256]{0,1:T(8,128)(2,1)S(1)}, u32[]{:S(2)}, u32[]{:S(2)}) %collective-permute-start.20) | collective-permute-done | bytes 524320 | tf_op jit(solution)/shard_map/ppermute | solution.py:21
  422.6 15.2 %convolution_convert_fusion = bf16[1024,6144]{1,0:T(8,128)(2,1)} fusion(bf16[6144,256]{1,0:T(8,128)(2,1)} %constant_dynamic-update-slice_fusion, bf16[6144,256]{1,0:T(8,128)(2,1)} %constant_dynamic-update-slice_fusion.4, bf16[6144,256]{1,0:T(8,128)(2,1)} %constant_dynamic-update-slice_fusion.8, bf16[1024,256]{0,1:T(8,128)(2,1)S(1)} %fusion.17, ...), kind=kOutput, calls=%fused_computation | convolution fusion | flops 9702998016 | bytes 23592960 | tf_op jit(solution)/shard_map/dot_general | solution.py:8
  453.5 76.4 %reduce-scatter.5.cloned.1.call-done = bf16[1024,768]{1,0:T(8,128)(2,1)} async-done(((bf16[1024,6144]{1,0:T(8,128)(2,1)}), bf16[1024,768]{1,0:T(8,128)(2,1)}) %reduce-scatter.5.cloned.1.call-update) | async-done | bytes 1572880 | tf_op jit(solution)/shard_map/reduce_scatter | solution.py:103
  (134 shorter events, 103.0 us)
Async XLA Ops:
  7.2 115.8 %all-gather.3.cloned.1.call-start = ((), (), s32[]{:S(2)}) async-start(), calls=%async_computation.3 | async-start | bytes 9437184 | tf_op jit(solution)/shard_map/all_gather | solution.py:76
  7.9 294.2 %all-gather.5.cloned.1.call-start = ((), (), s32[]{:S(2)}) async-start(), calls=%async_computation.4 | async-start | bytes 14155776 | tf_op jit(solution)/shard_map/all_gather | solution.py:79
  7.9 40.6 %collective-permute-start.1 = (bf16[1024,768]{1,0:T(8,128)(2,1)}, bf16[1024,768]{1,0:T(8,128)(2,1)S(1)}, u32[]{:S(2)}, u32[]{:S(2)}) collective-permute-start(bf16[1024,768]{1,0:T(8,128)(2,1)} %param.6), channel_id=1, source_target_pairs={{0,24},{8,16},{16,8},{24,0},{1,25},{9,17},{17,9},{25,1},{2,26},{10... | collective-permute-start | bytes 4718600 | tf_op jit(solution)/shard_map/ppermute | solution.py:21
  13.1 74.2 %collective-permute-start = (bf16[1024,768]{1,0:T(8,128)(2,1)}, bf16[1024,768]{1,0:T(8,128)(2,1)S(1)}, u32[]{:S(2)}, u32[]{:S(2)}) collective-permute-start(bf16[1024,768]{1,0:T(8,128)(2,1)} %param.6), channel_id=1, source_target_pairs={{0,8},{8,0},{16,24},{24,16},{1,9},{9,1},{17,25},{25,17},{2,10},{10... | collective-permute-start | bytes 4718600 | tf_op jit(solution)/shard_map/ppermute | solution.py:21
  53.8 66.6 %collective-permute-start.2 = (bf16[1024,768]{1,0:T(8,128)(2,1)}, bf16[1024,768]{1,0:T(8,128)(2,1)}, u32[]{:S(2)}, u32[]{:S(2)}) collective-permute-start(bf16[1024,768]{1,0:T(8,128)(2,1)} %get-tuple-element.29), channel_id=1, source_target_pairs={{0,16},{8,0},{16,24},{24,8},{1,17},{9,1},{17,25},{25,9},{2,18},{10... | collective-permute-start | bytes 4718600 | tf_op jit(solution)/shard_map/ppermute | solution.py:21
  135.1 302.7 %reduce-scatter.3.cloned.1.call-start = ((), (), s32[]{:S(2)}) async-start(), calls=%async_computation.2 | async-start | bytes 9437184 | tf_op jit(solution)/shard_map/reduce_scatter | solution.py:80
  139.0 22.5 %collective-permute-start.4 = (bf16[1536,256]{1,0:T(8,128)(2,1)}, bf16[1536,256]{1,0:T(8,128)(2,1)S(1)}, u32[]{:S(2)}, u32[]{:S(2)}) collective-permute-start(bf16[1536,256]{1,0:T(8,128)(2,1)} %get-tuple-element.18), channel_id=1, source_target_pairs={{0,24},{8,16},{16,8},{24,0},{1,25},{9,17},{17,9},{25,1},{2,26},{10... | collective-permute-start | bytes 2359304 | tf_op jit(solution)/shard_map/ppermute | solution.py:21
  141.2 71.1 %collective-permute-start.3 = (bf16[1536,256]{1,0:T(8,128)(2,1)}, bf16[1536,256]{1,0:T(8,128)(2,1)}, u32[]{:S(2)}, u32[]{:S(2)}) collective-permute-start(bf16[1536,256]{1,0:T(8,128)(2,1)} %get-tuple-element.18), channel_id=1, source_target_pairs={{0,8},{8,0},{16,24},{24,16},{1,9},{9,1},{17,25},{25,17},{2,10},{10... | collective-permute-start | bytes 2359304 | tf_op jit(solution)/shard_map/ppermute | solution.py:21
  165.2 51.9 %collective-permute-start.6 = (bf16[1536,256]{1,0:T(8,128)(2,1)}, bf16[1536,256]{1,0:T(8,128)(2,1)}, u32[]{:S(2)}, u32[]{:S(2)}) collective-permute-start(bf16[1536,256]{1,0:T(8,128)(2,1)} %get-tuple-element.17), channel_id=1, source_target_pairs={{0,8},{8,0},{16,24},{24,16},{1,9},{9,1},{17,25},{25,17},{2,10},{10... | collective-permute-start | bytes 2359304 | tf_op jit(solution)/shard_map/ppermute | solution.py:21
  180.0 54.6 %collective-permute-start.7 = (bf16[1536,256]{1,0:T(8,128)(2,1)}, bf16[1536,256]{1,0:T(8,128)(2,1)}, u32[]{:S(2)}, u32[]{:S(2)}) collective-permute-start(bf16[1536,256]{1,0:T(8,128)(2,1)} %get-tuple-element.17), channel_id=1, source_target_pairs={{0,24},{8,16},{16,8},{24,0},{1,25},{9,17},{17,9},{25,1},{2,26},{10... | collective-permute-start | bytes 2359304 | tf_op jit(solution)/shard_map/ppermute | solution.py:21
  182.2 52.5 %collective-permute-start.10 = (bf16[1536,256]{1,0:T(8,128)(2,1)}, bf16[1536,256]{1,0:T(8,128)(2,1)}, u32[]{:S(2)}, u32[]{:S(2)}) collective-permute-start(bf16[1536,256]{1,0:T(8,128)(2,1)} %get-tuple-element.16), channel_id=1, source_target_pairs={{0,24},{8,16},{16,8},{24,0},{1,25},{9,17},{17,9},{25,1},{2,26},{10... | collective-permute-start | bytes 2359304 | tf_op jit(solution)/shard_map/ppermute | solution.py:21
  195.7 334.2 %reduce-scatter.5.cloned.1.call-start = ((), (), s32[]{:S(2)}) async-start(), calls=%async_computation.5 | async-start | bytes 14155776 | tf_op jit(solution)/shard_map/reduce_scatter | solution.py:103
  212.3 45.6 %collective-permute-start.9 = (bf16[1536,256]{1,0:T(8,128)(2,1)}, bf16[1536,256]{1,0:T(8,128)(2,1)S(1)}, u32[]{:S(2)}, u32[]{:S(2)}) collective-permute-start(bf16[1536,256]{1,0:T(8,128)(2,1)} %get-tuple-element.16), channel_id=1, source_target_pairs={{0,8},{8,0},{16,24},{24,16},{1,9},{9,1},{17,25},{25,17},{2,10},{10... | collective-permute-start | bytes 2359304 | tf_op jit(solution)/shard_map/ppermute | solution.py:21
  212.3 55.2 %collective-permute-start.5 = (bf16[1536,256]{1,0:T(8,128)(2,1)}, bf16[1536,256]{1,0:T(8,128)(2,1)S(1)}, u32[]{:S(2)}, u32[]{:S(2)}) collective-permute-start(bf16[1536,256]{1,0:T(8,128)(2,1)} %get-tuple-element.14), channel_id=1, source_target_pairs={{0,16},{8,0},{16,24},{24,8},{1,17},{9,1},{17,25},{25,9},{2,18},{10... | collective-permute-start | bytes 2359304 | tf_op jit(solution)/shard_map/ppermute | solution.py:21
  239.5 44.9 %collective-permute-start.8 = (bf16[1536,256]{1,0:T(8,128)(2,1)S(1)}, bf16[1536,256]{1,0:T(8,128)(2,1)S(1)}, u32[]{:S(2)}, u32[]{:S(2)}) collective-permute-start(bf16[1536,256]{1,0:T(8,128)(2,1)S(1)} %get-tuple-element.20), channel_id=1, source_target_pairs={{0,16},{8,0},{16,24},{24,8},{1,17},{9,1},{17,25},{25,9},{2,18},{10... | collective-permute-start | bytes 2359304 | tf_op jit(solution)/shard_map/ppermute | solution.py:21
  257.9 43.2 %collective-permute-start.11 = (bf16[1536,256]{1,0:T(8,128)(2,1)S(1)}, bf16[1536,256]{1,0:T(8,128)(2,1)S(1)}, u32[]{:S(2)}, u32[]{:S(2)}) collective-permute-start(bf16[1536,256]{1,0:T(8,128)(2,1)S(1)} %get-tuple-element.22), channel_id=1, source_target_pairs={{0,16},{8,0},{16,24},{24,8},{1,17},{9,1},{17,25},{25,9},{2,18},{10... | collective-permute-start | bytes 2359304 | tf_op jit(solution)/shard_map/ppermute | solution.py:21
  316.7 26.4 %collective-permute-start.16 = (bf16[1024,256]{0,1:T(8,128)(2,1)S(1)}, bf16[1024,256]{0,1:T(8,128)(2,1)S(1)}, u32[]{:S(2)}, u32[]{:S(2)}) collective-permute-start(bf16[1024,256]{0,1:T(8,128)(2,1)S(1)} %get-tuple-element.26), channel_id=1, source_target_pairs={{0,8},{8,24},{16,0},{24,16},{1,9},{9,25},{17,1},{25,17},{2,10},{10... | collective-permute-start | bytes 1572872 | tf_op jit(solution)/shard_map/ppermute | solution.py:21
  328.1 17.5 %collective-permute-start.13 = (bf16[1024,256]{0,1:T(8,128)(2,1)S(1)}, bf16[1024,256]{0,1:T(8,128)(2,1)S(1)}, u32[]{:S(2)}, u32[]{:S(2)}) collective-permute-start(bf16[1024,256]{0,1:T(8,128)(2,1)S(1)} %get-tuple-element.24), channel_id=1, source_target_pairs={{0,8},{8,24},{16,0},{24,16},{1,9},{9,25},{17,1},{25,17},{2,10},{10... | collective-permute-start | bytes 1572872 | tf_op jit(solution)/shard_map/ppermute | solution.py:21
  341.0 26.3 %collective-permute-start.15 = (bf16[1024,256]{0,1:T(8,128)(2,1)S(1)}, bf16[1024,256]{0,1:T(8,128)(2,1)S(1)}, u32[]{:S(2)}, u32[]{:S(2)}) collective-permute-start(bf16[1024,256]{0,1:T(8,128)(2,1)S(1)} %get-tuple-element.25), channel_id=1, source_target_pairs={{0,8},{8,0},{16,24},{24,16},{1,9},{9,1},{17,25},{25,17},{2,10},{10... | collective-permute-start | bytes 1572872 | tf_op jit(solution)/shard_map/ppermute | solution.py:21
  343.3 35.3 %collective-permute-start.17 = (bf16[1024,256]{0,1:T(8,128)(2,1)S(1)}, bf16[1024,256]{0,1:T(8,128)(2,1)S(1)}, u32[]{:S(2)}, u32[]{:S(2)}) collective-permute-start(bf16[1024,256]{0,1:T(8,128)(2,1)S(1)} %fusion.18), channel_id=1, source_target_pairs={{0,24},{8,16},{16,8},{24,0},{1,25},{9,17},{17,9},{25,1},{2,26},{10... | collective-permute-start | bytes 1572872 | tf_op jit(solution)/shard_map/ppermute | solution.py:21
  345.5 42.9 %collective-permute-start.12 = (bf16[1024,256]{0,1:T(8,128)(2,1)S(1)}, bf16[1024,256]{0,1:T(8,128)(2,1)S(1)}, u32[]{:S(2)}, u32[]{:S(2)}) collective-permute-start(bf16[1024,256]{0,1:T(8,128)(2,1)S(1)} %get-tuple-element.23), channel_id=1, source_target_pairs={{0,8},{8,0},{16,24},{24,16},{1,9},{9,1},{17,25},{25,17},{2,10},{10... | collective-permute-start | bytes 1572872 | tf_op jit(solution)/shard_map/ppermute | solution.py:21
  345.5 67.1 %collective-permute-start.18 = (bf16[1024,256]{0,1:T(8,128)(2,1)S(1)}, bf16[1024,256]{0,1:T(8,128)(2,1)S(1)}, u32[]{:S(2)}, u32[]{:S(2)}) collective-permute-start(bf16[1024,256]{0,1:T(8,128)(2,1)S(1)} %get-tuple-element.27), channel_id=1, source_target_pairs={{0,8},{8,0},{16,24},{24,16},{1,9},{9,1},{17,25},{25,17},{2,10},{10... | collective-permute-start | bytes 1572872 | tf_op jit(solution)/shard_map/ppermute | solution.py:21
  356.6 55.6 %collective-permute-start.14 = (bf16[1024,256]{0,1:T(8,128)(2,1)S(1)}, bf16[1024,256]{0,1:T(8,128)(2,1)S(1)}, u32[]{:S(2)}, u32[]{:S(2)}) collective-permute-start(bf16[1024,256]{0,1:T(8,128)(2,1)S(1)} %fusion.22), channel_id=1, source_target_pairs={{0,24},{8,16},{16,8},{24,0},{1,25},{9,17},{17,9},{25,1},{2,26},{10... | collective-permute-start | bytes 1572872 | tf_op jit(solution)/shard_map/ppermute | solution.py:21
  367.3 54.9 %collective-permute-start.20 = (bf16[1024,256]{0,1:T(8,128)(2,1)S(1)}, bf16[1024,256]{0,1:T(8,128)(2,1)S(1)}, u32[]{:S(2)}, u32[]{:S(2)}) collective-permute-start(bf16[1024,256]{0,1:T(8,128)(2,1)S(1)} %fusion.14), channel_id=1, source_target_pairs={{0,24},{8,16},{16,8},{24,0},{1,25},{9,17},{17,9},{25,1},{2,26},{10... | collective-permute-start | bytes 1572872 | tf_op jit(solution)/shard_map/ppermute | solution.py:21
  (28 other events, 285.6 us)
Sparse Core Ops, SparseCore 0:
  9.9 57.0 all-gather.2
  135.2 73.1 all-gather.4
  211.9 71.2 reduce-scatter.2
  438.0 91.8 reduce-scatter.4

commit v3 on v1

v3 whole, which is shorter than its diff:
```python
import jax
import jax.numpy as jnp
from jax import lax
from jax.sharding import PartitionSpec as P

BF16 = jnp.bfloat16
F32 = jnp.float32

PAIRS = [(0, 1), (1, 0), (2, 3), (3, 2)]
MIDDLE = [(1, 2), (2, 1)]
OUTWARD = [(1, 0), (2, 3)]
INWARD = [(0, 1), (3, 2)]


def contract_last(first, second):
    return lax.dot_general(first, second, (((1,), (1,)), ((), ())), preferred_element_type=F32)


def contract_first(first, second):
    return lax.dot_general(first, second, (((0,), (0,)), ((), ())), preferred_element_type=F32)


def after(x, *earlier):
    return lax.optimization_barrier((x,) + earlier)[0]


def joined(keep_order, first, second):
    return jnp.where(keep_order, jnp.concatenate([first, second]), jnp.concatenate([second, first]))


def halves(keep_order, x):
    n = x.shape[0] // 2
    return jnp.where(keep_order, x[:n], x[n:]), jnp.where(keep_order, x[n:], x[:n])


class Line:
    def __init__(self, axis):
        self.axis = axis
        self.i = lax.axis_index(axis)
        self.even = self.i % 2 == 0
        self.lower = self.i < 2
        self.inner = (self.i == 1) | (self.i == 2)

    def send(self, x, pairs):
        return lax.ppermute(x, self.axis, pairs)

    def pair(self, x, *earlier):
        got = self.send(after(x, *earlier), PAIRS)
        return got, joined(self.even, x, got)

    def middle(self, near, *earlier):
        return self.send(after(near, *earlier), MIDDLE)

    def outward(self, middle, *earlier):
        return self.send(after(middle, *earlier), OUTWARD)

    def whole(self, near, middle, out):
        return joined(self.lower, near, jnp.where(self.inner, middle, out))

    def scatter_start(self, x):
        near, far = halves(self.lower, x)
        return near, far, self.send(far, INWARD)

    def scatter_end(self, near, through):
        got = self.send(through, MIDDLE)
        mine, other = halves(self.even, near.astype(F32) + got.astype(F32))
        got = self.send(other.astype(near.dtype), PAIRS)
        return (mine + got.astype(F32)).astype(near.dtype)


def add(first, second):
    return (first.astype(F32) + second.astype(F32)).astype(first.dtype)


def scatter_columns(rows, right_rel, axis):
    def swap(x, bit):
        return lax.ppermute(x, axis, [(j, j ^ bit) for j in range(8)])

    width = right_rel.shape[0] // 8
    kept = []
    cuts = 2
    size = rows.shape[0] // cuts
    for s in range(cuts):
        part = rows[s * size : (s + 1) * size]
        away = contract_last(part, right_rel[4 * width :]).astype(rows.dtype)
        here = contract_last(part, right_rel[: 4 * width])
        mine = (here + swap(away, 1).astype(F32)).astype(rows.dtype)
        half = size // 2
        block = lambda b, h: mine[h * half : (h + 1) * half, b * width : (b + 1) * width]
        by_x = swap(jnp.concatenate([block(1, 0), block(3, 0)], axis=1), 2)
        by_y = swap(jnp.concatenate([block(2, 1), block(3, 1)], axis=1), 4)
        then_y = swap(add(block(2, 0), by_x[:, width:]), 4)
        then_x = swap(add(block(1, 1), by_y[:, width:]), 2)
        kept.append(block(0, 0).astype(F32) + by_x[:, :width].astype(F32) + then_y.astype(F32))
        kept.append(block(0, 1).astype(F32) + by_y[:, :width].astype(F32) + then_x.astype(F32))
    return jnp.concatenate(kept).astype(rows.dtype)


def moments(rotated, first_moment, second_moment):
    first_next = 0.9 * first_moment + 0.1 * rotated
    second_next = 0.95 * second_moment + 0.05 * rotated * rotated
    scaled_first = first_next / (1.0 - 0.9**10)
    scaled_second = second_next / (1.0 - 0.95**10)
    normalized = (scaled_first / (jnp.sqrt(scaled_second) + 1e-08)).astype(BF16)
    return first_next, second_next, normalized


def cuts_of(width):
    sixth = width // 6
    ends = (0, 3 * sixth, 5 * sixth, width)
    return [slice(a, b) for a, b in zip(ends, ends[1:])]


def body_on_line(gradient, left_stat, left_basis, right_basis, first_moment, second_moment):
    line = Line("row")
    width = gradient.shape[1]
    cuts = cuts_of(width)
    left_cols = lax.all_gather(left_basis, "col", axis=0, tiled=True)
    items = [gradient[:, : width // 2], gradient[:, width // 2 :]] + [right_basis[:, cut] for cut in cuts]

    def left_rotated(columns):
        return lax.all_gather(contract_first(left_cols, columns).astype(BF16), "col", axis=1, tiled=True)

    pair0, near0 = line.pair(items[0])
    middle0 = line.middle(near0)
    pair1, near1 = line.pair(items[1], pair0)
    pair2, near2 = line.pair(items[2], pair1)
    out0 = line.outward(middle0, pair2)
    middle1 = line.middle(near1, middle0)
    columns0 = line.whole(near0, middle0, out0)
    rotated0 = left_rotated(columns0)
    pair3, near3 = line.pair(items[3], out0)
    out1 = line.outward(middle1, out0)
    middle2 = line.middle(near2, middle1)
    columns1 = line.whole(near1, middle1, out1)
    rotated1 = left_rotated(columns1)
    pair4, near4 = line.pair(items[4], out1)
    out2 = line.outward(middle2, out1)
    middle3 = line.middle(near3, middle2)
    out3 = line.outward(middle3, out2)
    middle4 = line.middle(near4, middle3)

    product = contract_last(jnp.concatenate([columns0, columns1], axis=1), gradient).astype(BF16)
    product = lax.psum_scatter(product, "col", scatter_dimension=0, tiled=True).astype(F32)
    left_next = 0.95 * left_stat + 0.05 * product

    first_out, second_out = [], []

    def part(cut, right_part, *earlier):
        split = right_part.reshape(8, 2, width // 2, right_part.shape[1])
        rotated = sum(
            jnp.dot(left, split[:, h].reshape(-1, right_part.shape[1]), preferred_element_type=F32)
            for h, left in enumerate((rotated0, rotated1))
        )
        first_next, second_next, normalized = moments(rotated, first_moment[:, cut], second_moment[:, cut])
        first_out.append(first_next)
        second_out.append(second_next)
        back = jnp.dot(left_cols, after(normalized, *earlier), preferred_element_type=F32).astype(BF16)
        return line.scatter_start(back)

    right0 = line.whole(near2, middle2, after(out2, middle4))
    back0, far0, sent0 = part(cuts[0], right0)
    out4 = line.outward(middle4, out3, far0)
    right1 = line.whole(near3, middle3, after(out3, far0))
    back1, far1, sent1 = part(cuts[1], right1, sent0)
    through0 = add(far0, sent0)
    right2 = line.whole(near4, middle4, after(out4, through0, far1))
    back2, far2, sent2 = part(cuts[2], right2, sent1)
    turned0 = line.scatter_end(back0, through0)
    turned1 = line.scatter_end(back1, add(far1, sent1))
    turned2 = line.scatter_end(back2, add(far2, sent2))

    i = lax.axis_index("col")
    right_cols = jnp.concatenate([right0, right1, right2], axis=1)
    blocks = [lax.dynamic_slice_in_dim(right_cols, (i ^ r) * width, width, 0) for r in (0, 2, 4, 6, 1, 3, 5, 7)]
    turned = jnp.concatenate([turned0, turned1, turned2], axis=1)
    direction = scatter_columns(turned, jnp.concatenate(blocks), "col")
    return (left_next, jnp.concatenate(first_out, axis=1), jnp.concatenate(second_out, axis=1), direction)


def body(gradient, left_stat, left_basis, right_basis, first_moment, second_moment):
    columns = lax.all_gather(gradient, "row", axis=0, tiled=True)
    left_cols = lax.all_gather(left_basis, "col", axis=0, tiled=True)
    right_cols = lax.all_gather(right_basis, "row", axis=0, tiled=True)
    left_rotated = lax.all_gather(contract_first(left_cols, columns).astype(BF16), "col", axis=1, tiled=True)
    product = contract_last(columns, gradient).astype(BF16)
    product = lax.psum_scatter(product, "col", scatter_dimension=0, tiled=True).astype(F32)
    left_next = 0.95 * left_stat + 0.05 * product
    rotated = jnp.dot(left_rotated, right_cols, preferred_element_type=F32)
    first_next, second_next, normalized = moments(rotated, first_moment, second_moment)
    back = jnp.dot(left_cols, normalized, preferred_element_type=F32).astype(BF16)
    back = lax.psum_scatter(back, "row", scatter_dimension=0, tiled=True)
    direction = contract_last(back, right_cols).astype(BF16)
    direction = lax.psum_scatter(direction, "col", scatter_dimension=1, tiled=True)
    return (left_next, first_next, second_next, direction)


def solution(mesh):
    on_line = mesh.shape["row"] == 4 and mesh.shape["col"] == 8
    return jax.shard_map(
        body_on_line if on_line else body,
        mesh=mesh,
        in_specs=(
            P("row", "col"),
            P("col", "row"),
            P("col", "row"),
            P("row", "col"),
            P("row", "col"),
            P("row", "col"),
        ),
        out_specs=(P("col", "row"), P("row", "col"), P("row", "col"), P("row", "col")),
        check_vma=False,
    )
```

time: 745 us -> 602 us (0.81)
  waiting for transfers between devices: 654 us -> 261 us
  starting transfers between devices: 0.46 us -> 103 us
  other arithmetic: 2.91 us -> 63.9 us
  matrix products: 69.6 us -> 109 us
  local copies, waits for them, and re-layouts: 3.85 us -> 42.4 us
    all_gather x4 -> x3, waiting for transfers between devices: 402 us -> 0.01 us  [the longest x2 0.01 us: left_rotated(): lax.all_gather(contract_first(left_cols, columns).astype(BF16), 'col', ax...]
    ppermute x0 -> x34, waiting for transfers between devices: none -> 261 us  [the longest x24 222 us: send(): return lax.ppermute(x, self.axis, pairs)]
    reduce_scatter x3 -> x1, waiting for transfers between devices: 250 us -> 0.01 us  [body_on_line(): lax.psum_scatter(product, 'col', scatter_dimension=0, tiled=True)]
    ppermute x0 -> x34, starting transfers between devices: none -> 103 us  [the longest x24 91.1 us: send(): return lax.ppermute(x, self.axis, pairs)]
    select_n x0 -> x18, other arithmetic: none -> 37.1 us  [the longest x10 28.9 us: joined(): jnp.where(keep_order, jnp.concatenate([first, second]), jnp.concatenate([...]
    unnamed x10 -> x96, local copies, waits for them, and re-layouts: 3.85 us -> 24.9 us
    dot_general x2 -> x9, matrix products: 29.4 us -> 49.5 us  [the longest x6 35 us: part(): jnp.dot(left, split[:, h].reshape(-1, right_part.shape[1]), preferred_ele...]
    dot_general x2 -> x5, matrix products: 28.3 us -> 46.4 us  [contract_last(): lax.dot_general(first, second, (((1,), (1,)), ((), ())), preferred_elemen...]
  transfers between devices with their start and end apart: 7 -> 38, of which waited for: 7 -> 15; matrix products, arithmetic and copies ran while one was open for 6% -> 33% of each run, Pallas kernels for 0% -> 0%
where the time goes in v3:
time: 602 us; the launch traced here: 595 us
  waiting for transfers between devices  261 us (43%)
  matrix products  109 us (18%)
  starting transfers between devices  103 us (17%)
  other arithmetic  63.9 us (11%)
  local copies, waits for them, and re-layouts  42.4 us (7%)
  between operations  15.1 us (3%)
    ppermute x24, waiting for transfers between devices, send(): return lax.ppermute(x, self.axis, pairs)  222 us
    ppermute x24, starting transfers between devices, send(): return lax.ppermute(x, self.axis, pairs)  91.1 us
    dot_general x5, matrix products, contract_last(): lax.dot_general(first, second, (((1,), (1,)), ((), ())), preferred_elemen...  46.4 us
    ppermute x10, waiting for transfers between devices, swap(): return lax.ppermute(x, axis, [(j, j ^ bit) for j in range(8)])  38.4 us
    dot_general x6, matrix products, part(): jnp.dot(left, split[:, h].reshape(-1, right_part.shape[1]), preferred_ele...  35 us
    select_n x10, other arithmetic, joined(): jnp.where(keep_order, jnp.concatenate([first, second]), jnp.concatenate([...  28.9 us
    unnamed x96, local copies, waits for them, and re-layouts  24.9 us
    dot_general x3, matrix products, part(): jnp.dot(left_cols, after(normalized, *earlier), preferred_element_type=F32)  14.5 us
  transfers between devices with their start and end apart: 38, of which 15 were waited for; matrix products, arithmetic and copies ran while one was open for 33% of the time, Pallas kernels for 0%

profile of v3, /device:TPU:0, one launch (start us, length us, event | category | flops | bytes accessed | tf_op | source)
XLA Modules:
  0.0 594.9 jit_solution(1676757458682972229)
XLA Ops:
  12.6 17.5 %collective-permute-done = bf16[1024,384]{1,0:T(8,128)(2,1)S(1)} collective-permute-done((bf16[1024,384]{1,0:T(8,128)(2,1)S(1)}, bf16[1024,384]{1,0:T(8,128)(2,1)S(1)}, u32[]{:S(2)}, u32[]{:S(2)}) %collective-permute-start) | collective-permute-done | bytes 786464 | tf_op jit(solution)/shard_map/ppermute | solution.py:45
  36.6 13.3 %collective-permute-done.2 = bf16[1024,384]{1,0:T(8,128)(2,1)} collective-permute-done((bf16[1024,384]{1,0:T(8,128)(2,1)S(1)}, bf16[1024,384]{1,0:T(8,128)(2,1)}, u32[]{:S(2)}, u32[]{:S(2)}) %collective-permute-start.2) | collective-permute-done | bytes 786464 | tf_op jit(solution)/shard_map/ppermute | solution.py:45
  51.4 24.9 %collective-permute-done.3 = bf16[1536,384]{1,0:T(8,128)(2,1)S(1)} collective-permute-done((bf16[1536,384]{1,0:T(8,128)(2,1)S(1)}, bf16[1536,384]{1,0:T(8,128)(2,1)S(1)}, u32[]{:S(2)}, u32[]{:S(2)}) %collective-permute-start.3) | collective-permute-done | bytes 1179680 | tf_op jit(solution)/shard_map/ppermute | solution.py:45
  78.6 34.7 %collective-permute-done.4 = bf16[2048,384]{1,0:T(8,128)(2,1)} collective-permute-done((bf16[2048,384]{1,0:T(8,128)(2,1)}, bf16[2048,384]{1,0:T(8,128)(2,1)}, u32[]{:S(2)}, u32[]{:S(2)}) %collective-permute-start.4) | collective-permute-done | bytes 1572896 | tf_op jit(solution)/shard_map/ppermute | solution.py:45
  114.9 8.3 %maximum_select_fusion.1 = bf16[4096,384]{1,0:T(8,128)(2,1)} fusion(bf16[2048,384]{1,0:T(8,128)(2,1)S(1)} %broadcast_select_fusion.4, bf16[2048,384]{1,0:T(8,128)(2,1)S(1)} %maximum_select_fusion.5, pred[]{:T(512)S(6)} %lt.33), kind=kLoop, calls=%fused_computation.18 | loop fusion | flops 14155776 | bytes 6291457 | tf_op jit(solution)/shard_map/jit(_where)/select_n | solution.py:28
  123.2 8.6 %fusion.7 = bf16[1024,384]{0,1:T(8,128)(2,1)} fusion(bf16[4096,384]{1,0:T(8,128)(2,1)} %maximum_select_fusion.1, bf16[4096,1024]{1,0:T(8,128)(2,1)} %all-gather.4.cloned.1.call-done), kind=kOutput, calls=%fused_computation.51 | convolution fusion | flops 3221618688 | bytes 12320768 | tf_op jit(solution)/shard_map/dot_general | solution.py:20
  135.9 63.7 %collective-permute-done.6 = bf16[2048,384]{1,0:T(8,128)(2,1)S(1)} collective-permute-done((bf16[2048,384]{1,0:T(8,128)(2,1)S(1)}, bf16[2048,384]{1,0:T(8,128)(2,1)S(1)}, u32[]{:S(2)}, u32[]{:S(2)}) %collective-permute-start.6) | collective-permute-done | bytes 1572896 | tf_op jit(solution)/shard_map/ppermute | solution.py:45
  199.8 7.2 %maximum_select_fusion.2 = bf16[4096,384]{1,0:T(8,128)(2,1)S(1)} fusion(bf16[2048,384]{1,0:T(8,128)(2,1)S(1)} %broadcast_select_fusion.3, bf16[2048,384]{1,0:T(8,128)(2,1)S(1)} %maximum_select_fusion.6, pred[]{:T(512)S(6)} %lt.33), kind=kLoop, calls=%fused_computation.19 | loop fusion | flops 14155776 | bytes 6291457 | tf_op jit(solution)/shard_map/jit(_where)/select_n | solution.py:28
  219.7 13.8 %collective-permute-done.10 = bf16[1536,256]{1,0:T(8,128)(2,1)S(1)} collective-permute-done((bf16[1536,256]{1,0:T(8,128)(2,1)S(1)}, bf16[1536,256]{1,0:T(8,128)(2,1)S(1)}, u32[]{:S(2)}, u32[]{:S(2)}) %collective-permute-start.10) | collective-permute-done | bytes 786464 | tf_op jit(solution)/shard_map/ppermute | solution.py:45
  239.0 32.5 %collective-permute-start.9 = (bf16[1536,128]{1,0:T(8,128)(2,1)}, bf16[1536,128]{1,0:T(8,128)(2,1)}, u32[]{:S(2)}, u32[]{:S(2)}) collective-permute-start(bf16[1536,128]{1,0:T(8,128)(2,1)} %slice.181), channel_id=1, source_target_pairs={{0,8},{8,0},{16,24},{24,16},{1,9},{9,1},{17,25},{25,17},{2,10},{10... | collective-permute-start | bytes 1179656 | tf_op jit(solution)/shard_map/ppermute | solution.py:45
  291.7 11.3 %convolution_convert_fusion = bf16[4096,1024]{1,0:T(8,128)(2,1)} fusion(bf16[1024,768]{1,0:T(8,128)(2,1)} %param.6, bf16[4096,384]{1,0:T(8,128)(2,1)} %copy-done.4, bf16[4096,384]{1,0:T(8,128)(2,1)} %maximum_select_fusion.1), kind=kOutput, calls=%fused_computation.1 | convolution fusion | flops 6459228160 | bytes 16252928 | tf_op jit(solution)/shard_map/dot_general | solution.py:16
  303.1 24.3 %collective-permute-done.8 = bf16[3072,384]{1,0:T(8,128)(2,1)} collective-permute-done((bf16[3072,384]{1,0:T(8,128)(2,1)}, bf16[3072,384]{1,0:T(8,128)(2,1)}, u32[]{:S(2)}, u32[]{:S(2)}) %collective-permute-start.8) | collective-permute-done | bytes 2359328 | tf_op jit(solution)/shard_map/ppermute | solution.py:45
  336.1 7.9 %fusion.31 = f32[1024,384]{0,1:T(8,128)} fusion(bf16[1024,3072]{0,1:T(8,128)(2,1)} %all-gather.6.cloned.1.call-done, bf16[3072,384]{1,0:T(8,128)(2,1)} %bitcast.52), kind=kOutput, calls=%fused_computation.106 | convolution fusion | flops 2415919104 | bytes 10223616 | tf_op jit(solution)/shard_map/dot_general | solution.py:152
  344.0 9.6 %divide_convert_fusion = (bf16[1024,384]{0,1:T(8,128)(2,1)S(1)}, f32[1024,384]{0,1:T(8,128)}, f32[1024,384]{0,1:T(8,128)}) fusion(f32[1024,384]{0,1:T(8,128)} %copy.18, f32[1024,384]{0,1:T(8,128)} %copy.20, f32[1024,384]{0,1:T(8,128)} %fusion.31, bf16[1024,3072]{0,1:T(8,128)(2,1)} %all-gather.8.cloned.1.call-done, bf16[3072,384]{1,0:T(8,128)(2,1)S(1)} %bitcast.51), kind=kOutput, calls=%fused_computation.41 | convolution fusion | flops 2421030912 | bytes 17301504 | tf_op jit(solution)/shard_map/dot_general | solution.py:152
  353.6 9.3 %fusion.3 = bf16[4096,384]{0,1:T(8,128)(2,1)S(1)} fusion(bf16[1024,384]{0,1:T(8,128)(2,1)S(1)} %get-tuple-element.50, bf16[4096,1024]{1,0:T(8,128)(2,1)} %all-gather.4.cloned.1.call-done), kind=kOutput, calls=%fused_computation.9 | convolution fusion | flops 3222798336 | bytes 12320768 | tf_op jit(solution)/shard_map/dot_general | solution.py:158
  383.1 10.6 %collective-permute-done.15 = bf16[2048,384]{0,1:T(8,128)(2,1)S(1)} collective-permute-done((bf16[2048,384]{0,1:T(8,128)(2,1)S(1)}, bf16[2048,384]{0,1:T(8,128)(2,1)S(1)}, u32[]{:S(2)}, u32[]{:S(2)}) %collective-permute-start.15) | collective-permute-done | bytes 1572896 | tf_op jit(solution)/shard_map/ppermute | solution.py:45
  433.1 8.8 %collective-permute-done.21 = bf16[2048,128]{0,1:T(8,128)(2,1)S(1)} collective-permute-done((bf16[2048,128]{0,1:T(8,128)(2,1)S(1)}, bf16[2048,128]{0,1:T(8,128)(2,1)S(1)}, u32[]{:S(2)}, u32[]{:S(2)}) %collective-permute-start.21) | collective-permute-done | bytes 524320 | tf_op jit(solution)/shard_map/ppermute | solution.py:45
  450.7 14.9 %collective-permute-start.23 = (bf16[1024,128]{0,1:T(8,128)(2,1)S(1)}, bf16[1024,128]{0,1:T(8,128)(2,1)S(1)}, u32[]{:S(2)}, u32[]{:S(2)}) collective-permute-start(bf16[1024,128]{0,1:T(8,128)(2,1)S(1)} %select_convert_fusion.2), channel_id=1, source_target_pairs={{0,8},{8,0},{16,24},{24,16},{1,9},{9,1},{17,25},{25,17},{2,10},{10... | collective-permute-start | bytes 786440 | tf_op jit(solution)/shard_map/ppermute | solution.py:45
  477.7 9.3 %convolution_convert_fusion.4 = bf16[512,3072]{1,0:T(8,128)(2,1)} fusion(bf16[768,768]{1,0:T(8,128)(2,1)S(1)} %get-tuple-element.54, bf16[768,768]{1,0:T(8,128)(2,1)S(1)} %copy-done.16, bf16[768,768]{1,0:T(8,128)(2,1)S(1)} %copy-done.17, bf16[768,768]{1,0:T(8,128)(2,1)S(1)} %copy-done.18, bf16[1024,768]{0,1:T(8,128)(2,1)S(1)} %pad_maximum_fusion.5), kind=kOutput, calls=%fused_computation.16 | convolution fusion | flops 2436366336 | bytes 8650752 | tf_op jit(solution)/shard_map/dot_general | solution.py:16
  487.1 8.0 %convolution_convert_fusion.5 = bf16[512,3072]{1,0:T(8,128)(2,1)S(1)} fusion(bf16[768,768]{1,0:T(8,128)(2,1)S(1)} %get-tuple-element.54, bf16[768,768]{1,0:T(8,128)(2,1)S(1)} %copy-done.16, bf16[768,768]{1,0:T(8,128)(2,1)S(1)} %copy-done.17, bf16[768,768]{1,0:T(8,128)(2,1)S(1)} %copy-done.18, bf16[1024,768]{0,1:T(8,128)(2,1)S(1)} %pad_maximum_fusion.5), kind=kOutput, calls=%fused_computation.17 | convolution fusion | flops 2436366336 | bytes 8650752 | tf_op jit(solution)/shard_map/dot_general | solution.py:16
  495.6 9.8 %add_convert_fusion = bf16[512,3072]{1,0:T(8,128)(2,1)S(1)} fusion(bf16[512,3072]{1,0:T(8,128)(2,1)} %collective-permute-done.29, bf16[768,768]{1,0:T(8,128)(2,1)S(1)} %copy-done.13, bf16[768,768]{1,0:T(8,128)(2,1)S(1)} %copy-done.14, bf16[768,768]{1,0:T(8,128)(2,1)S(1)} %copy-done.15, bf16[768,768]{1,0:T(8,128)(2,1)S(1)} %copy-done.12, ...), kind=kOutput, calls=%fused_computation.5 | convolution fusion | flops 2439512064 | bytes 11796480 | tf_op jit(solution)/shard_map/dot_general | solution.py:16
  507.6 8.1 %add_convert_fusion.1 = bf16[512,3072]{1,0:T(8,128)(2,1)S(1)} fusion(bf16[512,3072]{1,0:T(8,128)(2,1)S(1)} %collective-permute-done.24, bf16[768,768]{1,0:T(8,128)(2,1)S(1)} %copy-done.13, bf16[768,768]{1,0:T(8,128)(2,1)S(1)} %copy-done.14, bf16[768,768]{1,0:T(8,128)(2,1)S(1)} %copy-done.15, bf16[768,768]{1,0:T(8,128)(2,1)S(1)} %copy-done.12, ...), kind=kOutput, calls=%fused_computation.6 | convolution fusion | flops 2439512064 | bytes 11796480 | tf_op jit(solution)/shard_map/dot_general | solution.py:16
  528.2 14.1 %collective-permute-done.25 = bf16[256,1536]{1,0:T(8,128)(2,1)S(1)} collective-permute-done((bf16[256,1536]{1,0:T(8,128)(2,1)S(1)}, bf16[256,1536]{1,0:T(8,128)(2,1)S(1)}, u32[]{:S(2)}, u32[]{:S(2)}) %collective-permute-start.25) | collective-permute-done | bytes 786464 | tf_op jit(solution)/shard_map/ppermute | solution.py:77
  549.0 15.3 %collective-permute-done.31 = bf16[256,768]{1,0:T(8,128)(2,1)} collective-permute-done((bf16[256,768]{1,0:T(8,128)(2,1)S(1)}, bf16[256,768]{1,0:T(8,128)(2,1)}, u32[]{:S(2)}, u32[]{:S(2)}) %collective-permute-start.31) | collective-permute-done | bytes 393248 | tf_op jit(solution)/shard_map/ppermute | solution.py:77
  (237 shorter events, 193.9 us)
Async XLA Ops:
  7.2 116.0 %all-gather.4.cloned.1.call-start = ((), (), s32[]{:S(2)}) async-start(), calls=%async_computation.2 | async-start | bytes 9437184 | tf_op jit(solution)/shard_map/all_gather | solution.py:118
  7.9 328.2 %all-gather.6.cloned.1.call-start = ((), (), s32[]{:S(2)}) async-start(), calls=%async_computation.3 | async-start | bytes 7077888 | tf_op jit(solution)/shard_map/all_gather | solution.py:122
  49.9 26.3 %collective-permute-start.3 = (bf16[1536,384]{1,0:T(8,128)(2,1)S(1)}, bf16[1536,384]{1,0:T(8,128)(2,1)S(1)}, u32[]{:S(2)}, u32[]{:S(2)}) collective-permute-start(bf16[1536,384]{1,0:T(8,128)(2,1)S(1)} %slice.178), channel_id=1, source_target_pairs={{0,8},{8,0},{16,24},{24,16},{1,9},{9,1},{17,25},{25,17},{2,10},{10... | collective-permute-start | bytes 3538952 | tf_op jit(solution)/shard_map/ppermute | solution.py:45
  77.3 36.0 %collective-permute-start.4 = (bf16[2048,384]{1,0:T(8,128)(2,1)}, bf16[2048,384]{1,0:T(8,128)(2,1)}, u32[]{:S(2)}, u32[]{:S(2)}) collective-permute-start(bf16[2048,384]{1,0:T(8,128)(2,1)} %collective-permute-done.1), channel_id=1, source_target_pairs={{8,0},{16,24},{9,1},{17,25},{10,2},{18,26},{11,3},{19,27},{12,4},{... | collective-permute-start | bytes 4718600 | tf_op jit(solution)/shard_map/ppermute | solution.py:45
  131.9 212.2 %all-gather.8.cloned.1.call-start = ((), (), s32[]{:S(2)}) async-start(), calls=%async_computation.4 | async-start | bytes 7077888 | tf_op jit(solution)/shard_map/all_gather | solution.py:122
  134.4 65.2 %collective-permute-start.6 = (bf16[2048,384]{1,0:T(8,128)(2,1)S(1)}, bf16[2048,384]{1,0:T(8,128)(2,1)S(1)}, u32[]{:S(2)}, u32[]{:S(2)}) collective-permute-start(bf16[2048,384]{1,0:T(8,128)(2,1)S(1)} %collective-permute-done.5), channel_id=1, source_target_pairs={{8,0},{16,24},{9,1},{17,25},{10,2},{18,26},{11,3},{19,27},{12,4},{... | collective-permute-start | bytes 4718600 | tf_op jit(solution)/shard_map/ppermute | solution.py:45
  213.0 332.0 %reduce-scatter.2.cloned.1.call-start = ((), (), s32[]{:S(2)}) async-start(), calls=%async_computation.1 | async-start | bytes 9437184 | tf_op jit(solution)/shard_map/reduce_scatter | solution.py:144
  235.1 54.9 %collective-permute-start.11 = (bf16[3072,256]{1,0:T(8,128)(2,1)}, bf16[3072,256]{1,0:T(8,128)(2,1)}, u32[]{:S(2)}, u32[]{:S(2)}) collective-permute-start(bf16[3072,256]{1,0:T(8,128)(2,1)} %maximum_select_fusion.7), channel_id=1, source_target_pairs={{8,16},{16,8},{9,17},{17,9},{10,18},{18,10},{11,19},{19,11},{12,20... | collective-permute-start | bytes 4718600 | tf_op jit(solution)/shard_map/ppermute | solution.py:45
  239.0 49.3 %collective-permute-start.9 = (bf16[1536,128]{1,0:T(8,128)(2,1)}, bf16[1536,128]{1,0:T(8,128)(2,1)}, u32[]{:S(2)}, u32[]{:S(2)}) collective-permute-start(bf16[1536,128]{1,0:T(8,128)(2,1)} %slice.181), channel_id=1, source_target_pairs={{0,8},{8,0},{16,24},{24,16},{1,9},{9,1},{17,25},{25,17},{2,10},{10... | collective-permute-start | bytes 1179656 | tf_op jit(solution)/shard_map/ppermute | solution.py:45
  271.5 55.9 %collective-permute-start.8 = (bf16[3072,384]{1,0:T(8,128)(2,1)}, bf16[3072,384]{1,0:T(8,128)(2,1)}, u32[]{:S(2)}, u32[]{:S(2)}) collective-permute-start(bf16[3072,384]{1,0:T(8,128)(2,1)} %collective-permute-done.7), channel_id=1, source_target_pairs={{8,0},{16,24},{9,1},{17,25},{10,2},{18,26},{11,3},{19,27},{12,4},{... | collective-permute-start | bytes 7077896 | tf_op jit(solution)/shard_map/ppermute | solution.py:45
  290.0 38.7 %collective-permute-start.12 = (bf16[3072,128]{1,0:T(8,128)(2,1)S(1)}, bf16[3072,128]{1,0:T(8,128)(2,1)}, u32[]{:S(2)}, u32[]{:S(2)}) collective-permute-start(bf16[3072,128]{1,0:T(8,128)(2,1)S(1)} %maximum_select_fusion.9), channel_id=1, source_target_pairs={{8,16},{16,8},{9,17},{17,9},{10,18},{18,10},{11,19},{19,11},{12,20... | collective-permute-start | bytes 2359304 | tf_op jit(solution)/shard_map/ppermute | solution.py:45
  327.4 41.4 %collective-permute-start.13 = (bf16[3072,256]{1,0:T(8,128)(2,1)}, bf16[3072,256]{1,0:T(8,128)(2,1)}, u32[]{:S(2)}, u32[]{:S(2)}) collective-permute-start(bf16[3072,256]{1,0:T(8,128)(2,1)} %collective-permute-done.11), channel_id=1, source_target_pairs={{8,0},{16,24},{9,1},{17,25},{10,2},{18,26},{11,3},{19,27},{12,4},{... | collective-permute-start | bytes 4718600 | tf_op jit(solution)/shard_map/ppermute | solution.py:45
  363.1 30.6 %collective-permute-start.15 = (bf16[2048,384]{0,1:T(8,128)(2,1)S(1)}, bf16[2048,384]{0,1:T(8,128)(2,1)S(1)}, u32[]{:S(2)}, u32[]{:S(2)}) collective-permute-start(bf16[2048,384]{0,1:T(8,128)(2,1)S(1)} %broadcast_select_fusion.1), channel_id=1, source_target_pairs={{0,8},{24,16},{1,9},{25,17},{2,10},{26,18},{3,11},{27,19},{4,12},{... | collective-permute-start | bytes 4718600 | tf_op jit(solution)/shard_map/ppermute | solution.py:45
  368.8 40.5 %collective-permute-start.14 = (bf16[3072,128]{1,0:T(8,128)(2,1)}, bf16[3072,128]{1,0:T(8,128)(2,1)}, u32[]{:S(2)}, u32[]{:S(2)}) collective-permute-start(bf16[3072,128]{1,0:T(8,128)(2,1)} %collective-permute-done.12), channel_id=1, source_target_pairs={{8,0},{16,24},{9,1},{17,25},{10,2},{18,26},{11,3},{19,27},{12,4},{... | collective-permute-start | bytes 2359304 | tf_op jit(solution)/shard_map/ppermute | solution.py:45
  398.4 27.9 %collective-permute-start.18 = (bf16[2048,256]{0,1:T(8,128)(2,1)}, bf16[2048,256]{0,1:T(8,128)(2,1)}, u32[]{:S(2)}, u32[]{:S(2)}) collective-permute-start(bf16[2048,256]{0,1:T(8,128)(2,1)} %broadcast_select_fusion.5), channel_id=1, source_target_pairs={{0,8},{24,16},{1,9},{25,17},{2,10},{26,18},{3,11},{27,19},{4,12},{... | collective-permute-start | bytes 3145736 | tf_op jit(solution)/shard_map/ppermute | solution.py:45
  407.3 35.6 %collective-permute-start.16 = (bf16[2048,384]{0,1:T(8,128)(2,1)}, bf16[2048,384]{0,1:T(8,128)(2,1)}, u32[]{:S(2)}, u32[]{:S(2)}) collective-permute-start(bf16[2048,384]{0,1:T(8,128)(2,1)} %add_convert_fusion.2), channel_id=1, source_target_pairs={{8,16},{16,8},{9,17},{17,9},{10,18},{18,10},{11,19},{19,11},{12,20... | collective-permute-start | bytes 4718600 | tf_op jit(solution)/shard_map/ppermute | solution.py:45
  432.3 33.2 %collective-permute-start.19 = (bf16[2048,256]{0,1:T(8,128)(2,1)S(1)}, bf16[2048,256]{0,1:T(8,128)(2,1)S(1)}, u32[]{:S(2)}, u32[]{:S(2)}) collective-permute-start(bf16[2048,256]{0,1:T(8,128)(2,1)S(1)} %add_convert_fusion.3), channel_id=1, source_target_pairs={{8,16},{16,8},{9,17},{17,9},{10,18},{18,10},{11,19},{19,11},{12,20... | collective-permute-start | bytes 3145736 | tf_op jit(solution)/shard_map/ppermute | solution.py:45
  445.2 26.5 %collective-permute-start.17 = (bf16[1024,384]{0,1:T(8,128)(2,1)S(1)}, bf16[1024,384]{0,1:T(8,128)(2,1)S(1)}, u32[]{:S(2)}, u32[]{:S(2)}) collective-permute-start(bf16[1024,384]{0,1:T(8,128)(2,1)S(1)} %select_convert_fusion), channel_id=1, source_target_pairs={{0,8},{8,0},{16,24},{24,16},{1,9},{9,1},{17,25},{25,17},{2,10},{10... | collective-permute-start | bytes 2359304 | tf_op jit(solution)/shard_map/ppermute | solution.py:45
  450.7 20.9 %collective-permute-start.23 = (bf16[1024,128]{0,1:T(8,128)(2,1)S(1)}, bf16[1024,128]{0,1:T(8,128)(2,1)S(1)}, u32[]{:S(2)}, u32[]{:S(2)}) collective-permute-start(bf16[1024,128]{0,1:T(8,128)(2,1)S(1)} %select_convert_fusion.2), channel_id=1, source_target_pairs={{0,8},{8,0},{16,24},{24,16},{1,9},{9,1},{17,25},{25,17},{2,10},{10... | collective-permute-start | bytes 786440 | tf_op jit(solution)/shard_map/ppermute | solution.py:45
  515.9 26.3 %collective-permute-start.25 = (bf16[256,1536]{1,0:T(8,128)(2,1)S(1)}, bf16[256,1536]{1,0:T(8,128)(2,1)S(1)}, u32[]{:S(2)}, u32[]{:S(2)}) collective-permute-start(bf16[256,1536]{1,0:T(8,128)(2,1)S(1)} %pad_maximum_fusion.15), channel_id=1, source_target_pairs={{0,2},{1,3},{2,0},{3,1},{4,6},{5,7},{6,4},{7,5},{8,10},{9,11},{10,... | collective-permute-start | bytes 2359304 | tf_op jit(solution)/shard_map/ppermute | solution.py:77
  518.2 30.8 %collective-permute-start.32 = (bf16[256,1536]{1,0:T(8,128)(2,1)}, bf16[256,1536]{1,0:T(8,128)(2,1)}, u32[]{:S(2)}, u32[]{:S(2)}) collective-permute-start(bf16[256,1536]{1,0:T(8,128)(2,1)} %concatenate.131), channel_id=1, source_target_pairs={{0,4},{1,5},{2,6},{3,7},{4,0},{5,1},{6,2},{7,3},{8,12},{9,13},{10,... | collective-permute-start | bytes 2359304 | tf_op jit(solution)/shard_map/ppermute | solution.py:77
  520.3 47.8 %collective-permute-start.27 = (bf16[256,1536]{1,0:T(8,128)(2,1)}, bf16[256,1536]{1,0:T(8,128)(2,1)}, u32[]{:S(2)}, u32[]{:S(2)}) collective-permute-start(bf16[256,1536]{1,0:T(8,128)(2,1)} %concatenate.130), channel_id=1, source_target_pairs={{0,4},{1,5},{2,6},{3,7},{4,0},{5,1},{6,2},{7,3},{8,12},{9,13},{10,... | collective-permute-start | bytes 2359304 | tf_op jit(solution)/shard_map/ppermute | solution.py:77
  526.1 38.2 %collective-permute-start.31 = (bf16[256,768]{1,0:T(8,128)(2,1)S(1)}, bf16[256,768]{1,0:T(8,128)(2,1)}, u32[]{:S(2)}, u32[]{:S(2)}) collective-permute-start(bf16[256,768]{1,0:T(8,128)(2,1)S(1)} %add_convert_fusion.10), channel_id=1, source_target_pairs={{0,4},{1,5},{2,6},{3,7},{4,0},{5,1},{6,2},{7,3},{8,12},{9,13},{10,... | collective-permute-start | bytes 1179656 | tf_op jit(solution)/shard_map/ppermute | solution.py:77
  543.3 28.1 %collective-permute-start.26 = (bf16[256,768]{1,0:T(8,128)(2,1)}, bf16[256,768]{1,0:T(8,128)(2,1)}, u32[]{:S(2)}, u32[]{:S(2)}) collective-permute-start(bf16[256,768]{1,0:T(8,128)(2,1)} %add_convert_fusion.14), channel_id=1, source_target_pairs={{0,4},{1,5},{2,6},{3,7},{4,0},{5,1},{6,2},{7,3},{8,12},{9,13},{10,... | collective-permute-start | bytes 1179656 | tf_op jit(solution)/shard_map/ppermute | solution.py:77
  (61 other events, 801.6 us)
Sparse Core Ops, SparseCore 0:
  9.9 57.0 all-gather.3
  132.0 45.9 all-gather.5
  213.2 45.3 all-gather.7
  303.2 81.8 reduce-scatter.1

commit v4 on v3

--- a/solution.py
+++ b/solution.py
@@ -1,6 +1,7 @@
 import jax
 import jax.numpy as jnp
 from jax import lax
+from jax.experimental.layout import Layout, with_layout_constraint
 from jax.sharding import PartitionSpec as P
 
 BF16 = jnp.bfloat16
@@ -10,6 +11,9 @@
 MIDDLE = [(1, 2), (2, 1)]
 OUTWARD = [(1, 0), (2, 3)]
 INWARD = [(0, 1), (3, 2)]
+MIRROR = [(0, 3), (1, 2), (2, 1), (3, 0)]
+RELAY = [(0, 2), (1, 0), (2, 3), (3, 1)]
+RELAY_BACK = [(0, 1), (1, 3), (2, 0), (3, 2)]
 
 
 def contract_last(first, second):
@@ -20,8 +24,12 @@
     return lax.dot_general(first, second, (((0,), (0,)), ((), ())), preferred_element_type=F32)
 
 
+def together(operands, *earlier):
+    return lax.optimization_barrier(tuple(operands) + earlier)[: len(operands)]
+
+
 def after(x, *earlier):
-    return lax.optimization_barrier((x,) + earlier)[0]
+    return together([x], *earlier)[0]
 
 
 def joined(keep_order, first, second):
@@ -44,18 +52,18 @@
     def send(self, x, pairs):
         return lax.ppermute(x, self.axis, pairs)
 
-    def pair(self, x, *earlier):
-        got = self.send(after(x, *earlier), PAIRS)
-        return got, joined(self.even, x, got)
-
-    def middle(self, near, *earlier):
-        return self.send(after(near, *earlier), MIDDLE)
-
-    def outward(self, middle, *earlier):
-        return self.send(after(middle, *earlier), OUTWARD)
+    def near(self, x, got):
+        return joined(self.even, x, got)
 
     def whole(self, near, middle, out):
         return joined(self.lower, near, jnp.where(self.inner, middle, out))
+
+    def placed(self, whole, piece, bits):
+        return lax.dynamic_update_slice(whole, piece, ((self.i ^ bits) * piece.shape[0], 0))
+
+    def block(self, x, bits):
+        n = x.shape[0] // 4
+        return lax.dynamic_slice_in_dim(x, (self.i ^ bits) * n, n, 0)
 
     def scatter_start(self, x):
         near, far = halves(self.lower, x)
@@ -66,6 +74,14 @@
         mine, other = halves(self.even, near.astype(F32) + got.astype(F32))
         got = self.send(other.astype(near.dtype), PAIRS)
         return (mine + got.astype(F32)).astype(near.dtype)
+
+    def scatter_fast(self, x):
+        relay = self.send(self.block(x, 2), RELAY_BACK)
+        near = self.send(self.block(x, 1), PAIRS)
+        mirror = add(self.block(x, 3), jnp.where(self.inner, relay, 0))
+        mirror = self.send(mirror, MIRROR)
+        total = self.block(x, 0).astype(F32) + near.astype(F32) + jnp.where(self.inner, 0, relay).astype(F32)
+        return (total + mirror.astype(F32)).astype(x.dtype)
 
 
 def add(first, second):
@@ -82,9 +98,10 @@
     size = rows.shape[0] // cuts
     for s in range(cuts):
         part = rows[s * size : (s + 1) * size]
+        part = after(part, mine) if s else part
         away = contract_last(part, right_rel[4 * width :]).astype(rows.dtype)
-        here = contract_last(part, right_rel[: 4 * width])
-        mine = (here + swap(away, 1).astype(F32)).astype(rows.dtype)
+        here = contract_last(part, right_rel[: 4 * width]).astype(rows.dtype)
+        mine = add(after(here, away), swap(away, 1))
         half = size // 2
         block = lambda b, h: mine[h * half : (h + 1) * half, b * width : (b + 1) * width]
         by_x = swap(jnp.concatenate([block(1, 0), block(3, 0)], axis=1), 2)
@@ -105,77 +122,78 @@
     return first_next, second_next, normalized
 
 
-def cuts_of(width):
-    sixth = width // 6
-    ends = (0, 3 * sixth, 5 * sixth, width)
-    return [slice(a, b) for a, b in zip(ends, ends[1:])]
-
-
 def body_on_line(gradient, left_stat, left_basis, right_basis, first_moment, second_moment):
     line = Line("row")
-    width = gradient.shape[1]
-    cuts = cuts_of(width)
+    send = line.send
+    height, width = gradient.shape
+    cuts = [slice(p * width // 3, (p + 1) * width // 3) for p in range(3)]
     left_cols = lax.all_gather(left_basis, "col", axis=0, tiled=True)
-    items = [gradient[:, : width // 2], gradient[:, width // 2 :]] + [right_basis[:, cut] for cut in cuts]
-
-    def left_rotated(columns):
-        return lax.all_gather(contract_first(left_cols, columns).astype(BF16), "col", axis=1, tiled=True)
-
-    pair0, near0 = line.pair(items[0])
-    middle0 = line.middle(near0)
-    pair1, near1 = line.pair(items[1], pair0)
-    pair2, near2 = line.pair(items[2], pair1)
-    out0 = line.outward(middle0, pair2)
-    middle1 = line.middle(near1, middle0)
-    columns0 = line.whole(near0, middle0, out0)
-    rotated0 = left_rotated(columns0)
-    pair3, near3 = line.pair(items[3], out0)
-    out1 = line.outward(middle1, out0)
-    middle2 = line.middle(near2, middle1)
-    columns1 = line.whole(near1, middle1, out1)
-    rotated1 = left_rotated(columns1)
-    pair4, near4 = line.pair(items[4], out1)
-    out2 = line.outward(middle2, out1)
-    middle3 = line.middle(near3, middle2)
-    out3 = line.outward(middle3, out2)
-    middle4 = line.middle(near4, middle3)
-
-    product = contract_last(jnp.concatenate([columns0, columns1], axis=1), gradient).astype(BF16)
+    own0, own1, own2 = [right_basis[:, cut] for cut in cuts]
+
+    mirror = send(gradient, MIRROR)
+    pair = send(gradient, PAIRS)
+
+    relay, own0 = together([jnp.where(line.inner, mirror, gradient), own0], pair)
+    relay = send(relay, RELAY)
+    pair0 = send(own0, PAIRS)
+    columns = jnp.zeros((4 * height, width), BF16)
+    for bits, piece in ((0, gradient), (1, pair), (3, mirror)):
+        columns = line.placed(columns, piece, bits)
+
+    near0, own1, own2 = together([line.near(own0, pair0), own1, own2], relay)
+    middle0 = send(near0, MIDDLE)
+    pair1 = send(own1, PAIRS)
+    pair2 = send(own2, PAIRS)
+    columns = line.placed(columns, after(relay, pair1), 2)
+    left_part = contract_first(left_cols, columns).astype(BF16)
+    left_rotated = lax.all_gather(left_part, "col", axis=1, tiled=True)
+
+    middle0, near1 = together([middle0, line.near(own1, pair1)], pair2, left_part)
+    out0 = send(middle0, OUTWARD)
+    middle1 = send(near1, MIDDLE)
+    product = contract_last(after(columns, near1), gradient).astype(BF16)
+    product = after(product, left_rotated)
     product = lax.psum_scatter(product, "col", scatter_dimension=0, tiled=True).astype(F32)
     left_next = 0.95 * left_stat + 0.05 * product
 
+    middle1, near2 = together([middle1, line.near(own2, pair2)], out0)
+    out1 = send(middle1, OUTWARD)
+    middle2 = send(near2, MIDDLE)
+
     first_out, second_out = [], []
 
     def part(cut, right_part, *earlier):
-        split = right_part.reshape(8, 2, width // 2, right_part.shape[1])
-        rotated = sum(
-            jnp.dot(left, split[:, h].reshape(-1, right_part.shape[1]), preferred_element_type=F32)
-            for h, left in enumerate((rotated0, rotated1))
-        )
+        rotated = jnp.dot(left_rotated, right_part, preferred_element_type=F32)
         first_next, second_next, normalized = moments(rotated, first_moment[:, cut], second_moment[:, cut])
         first_out.append(first_next)
         second_out.append(second_next)
-        back = jnp.dot(left_cols, after(normalized, *earlier), preferred_element_type=F32).astype(BF16)
-        return line.scatter_start(back)
-
-    right0 = line.whole(near2, middle2, after(out2, middle4))
-    back0, far0, sent0 = part(cuts[0], right0)
-    out4 = line.outward(middle4, out3, far0)
-    right1 = line.whole(near3, middle3, after(out3, far0))
-    back1, far1, sent1 = part(cuts[1], right1, sent0)
+        return jnp.dot(left_cols, after(normalized, *earlier), preferred_element_type=F32).astype(BF16)
+
+    right0 = line.whole(near0, middle0, after(out0, near2))
+    back0, far0, sent0 = line.scatter_start(part(cuts[0], right0))
+    out2 = send(after(middle2, out1, far0), OUTWARD)
+    right1 = line.whole(near1, middle1, after(out1, far0))
+    back1, far1, sent1 = line.scatter_start(part(cuts[1], right1, sent0))
     through0 = add(far0, sent0)
-    right2 = line.whole(near4, middle4, after(out4, through0, far1))
-    back2, far2, sent2 = part(cuts[2], right2, sent1)
+    right2 = line.whole(near2, middle2, after(out2, through0, far1))
+    back2 = part(cuts[2], right2, sent1)
+    turned2 = line.scatter_fast(back2)
     turned0 = line.scatter_end(back0, through0)
     turned1 = line.scatter_end(back1, add(far1, sent1))
-    turned2 = line.scatter_end(back2, add(far2, sent2))
 
     i = lax.axis_index("col")
-    right_cols = jnp.concatenate([right0, right1, right2], axis=1)
+    right_cols = jnp.concatenate(together([right0, right1, right2], back2), axis=1)
     blocks = [lax.dynamic_slice_in_dim(right_cols, (i ^ r) * width, width, 0) for r in (0, 2, 4, 6, 1, 3, 5, 7)]
+    first_next, second_next = [
+        with_layout_constraint(jnp.concatenate(together(x, back2), axis=1), Layout((0, 1)))
+        for x in (first_out, second_out)
+    ]
     turned = jnp.concatenate([turned0, turned1, turned2], axis=1)
-    direction = scatter_columns(turned, jnp.concatenate(blocks), "col")
-    return (left_next, jnp.concatenate(first_out, axis=1), jnp.concatenate(second_out, axis=1), direction)
+    turned, right_rel, left_next, first_next, second_next = together(
+        [turned, jnp.concatenate(blocks), left_next, first_next, second_next]
+    )
+    direction = scatter_columns(turned, right_rel, "col")
+    return (left_next, first_next, second_next, direction)
 
 
 def body(gradient, left_stat, left_basis, right_basis, first_moment, second_moment):

time: 602 us -> 510 us (0.85)
  other arithmetic: 63.9 us -> 39.5 us
  starting transfers between devices: 103 us -> 83.6 us
  local copies, waits for them, and re-layouts: 42.4 us -> 24.4 us
  matrix products: 109 us -> 93.4 us
  waiting for transfers between devices: 261 us -> 247 us
    ppermute x24 -> x21, waiting for transfers between devices: 222 us -> 193 us  [send(): return lax.ppermute(x, self.axis, pairs)]
    ppermute x24 -> x21, starting transfers between devices: 91.1 us -> 71.9 us  [send(): return lax.ppermute(x, self.axis, pairs)]
    unnamed x96 -> x27, local copies, waits for them, and re-layouts: 24.9 us -> 9.31 us
    select_n x10 -> x6, other arithmetic: 28.9 us -> 13.9 us  [joined(): jnp.where(keep_order, jnp.concatenate([first, second]), jnp.concatenate([...]
    ppermute x10, waiting for transfers between devices: 38.4 us -> 53.3 us  [swap(): return lax.ppermute(x, axis, [(j, j ^ bit) for j in range(8)])]
    dot_general x5, matrix products: 46.4 us -> 33.1 us  [contract_last(): lax.dot_general(first, second, (((1,), (1,)), ((), ())), preferred_elemen...]
    slice x16 -> x2, local copies, waits for them, and re-layouts: 11.8 us -> 2.99 us  [the longest x1 2.92 us: body_on_line(): own0, own1, own2 = [right_basis[:, cut] for cut in cuts]]
    another operation x4, other arithmetic: 7.41 us -> 0.79 us
  transfers between devices with their start and end apart: 38 -> 34, of which waited for: 15 -> 16; matrix products, arithmetic and copies ran while one was open for 33% -> 25% of each run, Pallas kernels for 0% -> 0%
where the time goes in v4:
time: 510 us; the launch traced here: 503 us
  waiting for transfers between devices  247 us (48%)
  matrix products  93.4 us (18%)
  starting transfers between devices  83.6 us (16%)
  other arithmetic  39.5 us (8%)
  local copies, waits for them, and re-layouts  24.4 us (5%)
  between operations  14.5 us (3%)
    ppermute x21, waiting for transfers between devices, send(): return lax.ppermute(x, self.axis, pairs)  193 us
    ppermute x21, starting transfers between devices, send(): return lax.ppermute(x, self.axis, pairs)  71.9 us
    ppermute x10, waiting for transfers between devices, swap(): return lax.ppermute(x, axis, [(j, j ^ bit) for j in range(8)])  53.3 us
    dot_general x5, matrix products, contract_last(): lax.dot_general(first, second, (((1,), (1,)), ((), ())), preferred_elemen...  33.1 us
    dot_general x3, matrix products, part(): rotated = jnp.dot(left_rotated, right_part, preferred_element_type=F32)  29.2 us
    dot_general x3, matrix products, part(): jnp.dot(left_cols, after(normalized, *earlier), preferred_element_type=F32)  18.9 us
    select_n x6, other arithmetic, joined(): jnp.where(keep_order, jnp.concatenate([first, second]), jnp.concatenate([...  13.9 us
    dot_general x1, matrix products, contract_first(): lax.dot_general(first, second, (((0,), (0,)), ((), ())), preferred_elemen...  12.1 us
  transfers between devices with their start and end apart: 34, of which 16 were waited for; matrix products, arithmetic and copies ran while one was open for 25% of the time, Pallas kernels for 0%

profile of v4, /device:TPU:0, one launch (start us, length us, event | category | flops | bytes accessed | tf_op | source)
XLA Modules:
  0.0 502.7 jit_solution(1812009595093659261)
XLA Ops:
  16.0 32.6 %collective-permute-done.1 = bf16[1024,768]{1,0:T(8,128)(2,1)S(1)} collective-permute-done((bf16[1024,768]{1,0:T(8,128)(2,1)}, bf16[1024,768]{1,0:T(8,128)(2,1)S(1)}, u32[]{:S(2)}, u32[]{:S(2)}) %collective-permute-start.1) | collective-permute-done | bytes 1572896 | tf_op jit(solution)/shard_map/ppermute | solution.py:53
  53.8 27.8 %collective-permute-done = bf16[1024,768]{1,0:T(8,128)(2,1)} collective-permute-done((bf16[1024,768]{1,0:T(8,128)(2,1)}, bf16[1024,768]{1,0:T(8,128)(2,1)}, u32[]{:S(2)}, u32[]{:S(2)}) %collective-permute-start) | collective-permute-done | bytes 1572896 | tf_op jit(solution)/shard_map/ppermute | solution.py:53
  87.3 50.0 %collective-permute-done.3 = bf16[1536,256]{1,0:T(8,128)(2,1)} collective-permute-done((bf16[1536,256]{1,0:T(8,128)(2,1)S(1)}, bf16[1536,256]{1,0:T(8,128)(2,1)}, u32[]{:S(2)}, u32[]{:S(2)}) %collective-permute-start.3) | collective-permute-done | bytes 786464 | tf_op jit(solution)/shard_map/ppermute | solution.py:53
  146.1 12.3 %collective-permute-done.4 = bf16[1536,256]{1,0:T(8,128)(2,1)} collective-permute-done((bf16[1536,256]{1,0:T(8,128)(2,1)}, bf16[1536,256]{1,0:T(8,128)(2,1)}, u32[]{:S(2)}, u32[]{:S(2)}) %collective-permute-start.4) | collective-permute-done | bytes 786464 | tf_op jit(solution)/shard_map/ppermute | solution.py:53
  161.0 12.1 %fusion.6 = bf16[1024,768]{0,1:T(8,128)(2,1)} fusion(bf16[4096,768]{1,0:T(8,128)(2,1)} %constant_dynamic-update-slice_fusion.3, bf16[4096,1024]{1,0:T(8,128)(2,1)} %all-gather.3.cloned.1.call-done), kind=kOutput, calls=%fused_computation.39 | convolution fusion | flops 6443237376 | bytes 16252928 | tf_op jit(solution)/shard_map/dot_general | solution.py:24
  180.2 12.6 %collective-permute-done.6 = bf16[1536,256]{1,0:T(8,128)(2,1)} collective-permute-done((bf16[1536,256]{1,0:T(8,128)(2,1)}, bf16[1536,256]{1,0:T(8,128)(2,1)}, u32[]{:S(2)}, u32[]{:S(2)}) %collective-permute-start.6) | collective-permute-done | bytes 786464 | tf_op jit(solution)/shard_map/ppermute | solution.py:53
  199.5 11.8 %convolution_convert_fusion = bf16[4096,1024]{1,0:T(8,128)(2,1)} fusion(bf16[4096,768]{1,0:T(8,128)(2,1)} %constant_dynamic-update-slice_fusion.3, bf16[1024,768]{1,0:T(8,128)(2,1)S(1)} %copy-done.5), kind=kOutput, calls=%fused_computation | convolution fusion | flops 6446645248 | bytes 16252928 | tf_op jit(solution)/shard_map/dot_general | solution.py:20
  211.3 34.3 %collective-permute-done.7 = bf16[3072,256]{1,0:T(8,128)(2,1)S(1)} collective-permute-done((bf16[3072,256]{1,0:T(8,128)(2,1)}, bf16[3072,256]{1,0:T(8,128)(2,1)S(1)}, u32[]{:S(2)}, u32[]{:S(2)}) %collective-permute-start.7) | collective-permute-done | bytes 1572896 | tf_op jit(solution)/shard_map/ppermute | solution.py:53
  251.6 9.1 %divide_convert_fusion.2 = (bf16[1024,256]{1,0:T(8,128)(2,1)S(1)}, f32[1024,256]{1,0:T(8,128)S(1)}, f32[1024,256]{1,0:T(8,128)S(1)}) fusion(f32[1024,768]{1,0:T(8,128)} %param.10, f32[1024,768]{1,0:T(8,128)} %param.11, bf16[1024,6144]{0,1:T(8,128)(2,1)} %all-gather.5.cloned.1.call-done, bf16[6144,256]{1,0:T(8,128)(2,1)S(1)} %maximum_select_fusion), kind=kOutput, calls=%fused_computation.65 | convolution fusion | flops 3224371200 | bytes 20447232 | tf_op jit(solution)/shard_map/dot_general | solution.py:166
  260.7 7.0 %fusion = bf16[4096,256]{0,1:T(8,128)(2,1)S(1)} fusion(bf16[1024,256]{1,0:T(8,128)(2,1)S(1)} %get-tuple-element.80, bf16[4096,1024]{1,0:T(8,128)(2,1)} %all-gather.3.cloned.1.call-done), kind=kOutput, calls=%fused_computation.6 | convolution fusion | flops 2148532224 | bytes 11010048 | tf_op jit(solution)/shard_map/dot_general | solution.py:170
  267.8 7.6 %collective-permute-start.9 = (bf16[2048,256]{0,1:T(8,128)(2,1)S(1)}, bf16[2048,256]{0,1:T(8,128)(2,1)S(1)}, u32[]{:S(2)}, u32[]{:S(2)}) collective-permute-start(bf16[2048,256]{0,1:T(8,128)(2,1)S(1)} %broadcast_select_fusion.5), channel_id=1, source_target_pairs={{0,8},{24,16},{1,9},{25,17},{2,10},{26,18},{3,11},{27,19},{4,12},{... | collective-permute-start | bytes 3145736 | tf_op jit(solution)/shard_map/ppermute | solution.py:53
  275.5 6.1 %collective-permute-done.12 = bf16[3072,256]{1,0:T(8,128)(2,1)} collective-permute-done((bf16[3072,256]{1,0:T(8,128)(2,1)}, bf16[3072,256]{1,0:T(8,128)(2,1)}, u32[]{:S(2)}, u32[]{:S(2)}) %collective-permute-start.12) | collective-permute-done | bytes 1572896 | tf_op jit(solution)/shard_map/ppermute | solution.py:53
  285.8 9.7 %divide_convert_fusion.1 = (bf16[1024,256]{1,0:T(8,128)(2,1)S(1)}, f32[1024,256]{1,0:T(8,128)S(1)}, f32[1024,256]{1,0:T(8,128)S(1)}) fusion(f32[1024,768]{1,0:T(8,128)} %param.10, f32[1024,768]{1,0:T(8,128)} %param.11, bf16[1024,6144]{0,1:T(8,128)(2,1)} %all-gather.5.cloned.1.call-done, bf16[6144,256]{1,0:T(8,128)(2,1)S(1)} %maximum_select_fusion.1), kind=kOutput, calls=%fused_computation.61 | convolution fusion | flops 3224371200 | bytes 20447232 | tf_op jit(solution)/shard_map/dot_general | solution.py:166
  298.7 6.0 %fusion.1 = bf16[4096,256]{0,1:T(8,128)(2,1)S(1)} fusion(bf16[1024,256]{1,0:T(8,128)(2,1)S(1)} %get-tuple-element.51, bf16[4096,1024]{1,0:T(8,128)(2,1)} %all-gather.3.cloned.1.call-done), kind=kOutput, calls=%fused_computation.7 | convolution fusion | flops 2148532224 | bytes 11010048 | tf_op jit(solution)/shard_map/dot_general | solution.py:170
  304.8 6.0 %collective-permute-start.13 = (bf16[2048,256]{0,1:T(8,128)(2,1)S(1)}, bf16[2048,256]{0,1:T(8,128)(2,1)S(1)}, u32[]{:S(2)}, u32[]{:S(2)}) collective-permute-start(bf16[2048,256]{0,1:T(8,128)(2,1)S(1)} %broadcast_select_fusion.4), channel_id=1, source_target_pairs={{0,8},{24,16},{1,9},{25,17},{2,10},{26,18},{3,11},{27,19},{4,12},{... | collective-permute-start | bytes 3145736 | tf_op jit(solution)/shard_map/ppermute | solution.py:53
  310.8 6.4 %collective-permute-done.17 = bf16[3072,256]{1,0:T(8,128)(2,1)S(1)} collective-permute-done((bf16[3072,256]{1,0:T(8,128)(2,1)}, bf16[3072,256]{1,0:T(8,128)(2,1)S(1)}, u32[]{:S(2)}, u32[]{:S(2)}) %collective-permute-start.17) | collective-permute-done | bytes 1572896 | tf_op jit(solution)/shard_map/ppermute | solution.py:53
  319.7 10.4 %divide_convert_fusion = (bf16[1024,256]{1,0:T(8,128)(2,1)S(1)}, f32[1024,256]{1,0:T(8,128)S(1)}, f32[1024,256]{1,0:T(8,128)}) fusion(f32[1024,768]{1,0:T(8,128)} %param.10, f32[1024,768]{1,0:T(8,128)} %param.11, bf16[1024,6144]{0,1:T(8,128)(2,1)} %all-gather.5.cloned.1.call-done, bf16[6144,256]{1,0:T(8,128)(2,1)S(1)} %maximum_select_fusion.2), kind=kOutput, calls=%fused_computation.57 | convolution fusion | flops 3224371200 | bytes 20447232 | tf_op jit(solution)/shard_map/dot_general | solution.py:166
  334.8 6.0 %convolution_convert_fusion.1 = bf16[256,4096]{1,0:T(8,128)(2,1)S(1)} fusion(bf16[1024,256]{1,0:T(8,128)(2,1)S(1)} %get-tuple-element.54, bf16[4096,1024]{1,0:T(8,128)(2,1)} %all-gather.3.cloned.1.call-done), kind=kOutput, calls=%fused_computation.3 | convolution fusion | flops 2148532224 | bytes 11010048 | tf_op jit(solution)/shard_map/dot_general | solution.py:170
  359.8 5.7 %collective-permute-done.19 = bf16[1024,256]{0,1:T(8,128)(2,1)S(1)} collective-permute-done((bf16[1024,256]{0,1:T(8,128)(2,1)}, bf16[1024,256]{0,1:T(8,128)(2,1)S(1)}, u32[]{:S(2)}, u32[]{:S(2)}) %collective-permute-start.19) | collective-permute-done | bytes 524320 | tf_op jit(solution)/shard_map/ppermute | solution.py:53
  367.6 25.5 %collective-permute-start.15 = (bf16[1024,256]{0,1:T(8,128)(2,1)S(1)}, bf16[1024,256]{0,1:T(8,128)(2,1)S(1)}, u32[]{:S(2)}, u32[]{:S(2)}) collective-permute-start(bf16[1024,256]{0,1:T(8,128)(2,1)S(1)} %select_convert_fusion), channel_id=1, source_target_pairs={{0,8},{8,0},{16,24},{24,16},{1,9},{9,1},{17,25},{25,17},{2,10},{10... | collective-permute-start | bytes 1572872 | tf_op jit(solution)/shard_map/ppermute | solution.py:53
  433.6 9.4 %collective-permute-done.22 = bf16[256,1536]{1,0:T(8,128)(2,1)S(1)} collective-permute-done((bf16[256,1536]{1,0:T(8,128)(2,1)S(1)}, bf16[256,1536]{1,0:T(8,128)(2,1)S(1)}, u32[]{:S(2)}, u32[]{:S(2)}) %collective-permute-start.22) | collective-permute-done | bytes 786464 | tf_op jit(solution)/shard_map/ppermute | solution.py:93
  444.9 14.3 %collective-permute-done.27 = bf16[256,1536]{1,0:T(8,128)(2,1)S(1)} collective-permute-done((bf16[256,1536]{1,0:T(8,128)(2,1)S(1)}, bf16[256,1536]{1,0:T(8,128)(2,1)S(1)}, u32[]{:S(2)}, u32[]{:S(2)}) %collective-permute-start.27) | collective-permute-done | bytes 786464 | tf_op jit(solution)/shard_map/ppermute | solution.py:93
  461.1 16.1 %collective-permute-done.23 = bf16[256,768]{1,0:T(8,128)(2,1)S(1)} collective-permute-done((bf16[256,768]{1,0:T(8,128)(2,1)S(1)}, bf16[256,768]{1,0:T(8,128)(2,1)S(1)}, u32[]{:S(2)}, u32[]{:S(2)}) %collective-permute-start.23) | collective-permute-done | bytes 393248 | tf_op jit(solution)/shard_map/ppermute | solution.py:93
  486.5 8.0 %collective-permute-done.30 = bf16[256,768]{1,0:T(8,128)(2,1)S(1)} collective-permute-done((bf16[256,768]{1,0:T(8,128)(2,1)S(1)}, bf16[256,768]{1,0:T(8,128)(2,1)S(1)}, u32[]{:S(2)}, u32[]{:S(2)}) %collective-permute-start.30) | collective-permute-done | bytes 393248 | tf_op jit(solution)/shard_map/ppermute | solution.py:93
  (135 shorter events, 141.4 us)
Async XLA Ops:
  7.2 153.8 %all-gather.3.cloned.1.call-start = ((), (), s32[]{:S(2)}) async-start(), calls=%async_computation.1 | async-start | bytes 9437184 | tf_op jit(solution)/shard_map/all_gather | solution.py:130
  7.9 243.6 %all-gather.5.cloned.1.call-start = ((), (), s32[]{:S(2)}) async-start(), calls=%async_computation.2 | async-start | bytes 14155776 | tf_op jit(solution)/shard_map/all_gather | solution.py:149
  7.9 40.6 %collective-permute-start.1 = (bf16[1024,768]{1,0:T(8,128)(2,1)}, bf16[1024,768]{1,0:T(8,128)(2,1)S(1)}, u32[]{:S(2)}, u32[]{:S(2)}) collective-permute-start(bf16[1024,768]{1,0:T(8,128)(2,1)} %param.6), channel_id=1, source_target_pairs={{0,24},{8,16},{16,8},{24,0},{1,25},{9,17},{17,9},{25,1},{2,26},{10... | collective-permute-start | bytes 4718600 | tf_op jit(solution)/shard_map/ppermute | solution.py:53
  13.1 68.5 %collective-permute-start = (bf16[1024,768]{1,0:T(8,128)(2,1)}, bf16[1024,768]{1,0:T(8,128)(2,1)}, u32[]{:S(2)}, u32[]{:S(2)}) collective-permute-start(bf16[1024,768]{1,0:T(8,128)(2,1)} %param.6), channel_id=1, source_target_pairs={{0,8},{8,0},{16,24},{24,16},{1,9},{9,1},{17,25},{25,17},{2,10},{10... | collective-permute-start | bytes 4718600 | tf_op jit(solution)/shard_map/ppermute | solution.py:53
  81.6 57.9 %collective-permute-start.2 = (bf16[1024,768]{1,0:T(8,128)(2,1)}, bf16[1024,768]{1,0:T(8,128)(2,1)}, u32[]{:S(2)}, u32[]{:S(2)}) collective-permute-start(bf16[1024,768]{1,0:T(8,128)(2,1)} %get-tuple-element.39), channel_id=1, source_target_pairs={{0,16},{8,0},{16,24},{24,8},{1,17},{9,1},{17,25},{25,9},{2,18},{10... | collective-permute-start | bytes 4718600 | tf_op jit(solution)/shard_map/ppermute | solution.py:53
  87.3 50.0 %collective-permute-start.3 = (bf16[1536,256]{1,0:T(8,128)(2,1)S(1)}, bf16[1536,256]{1,0:T(8,128)(2,1)}, u32[]{:S(2)}, u32[]{:S(2)}) collective-permute-start(bf16[1536,256]{1,0:T(8,128)(2,1)S(1)} %get-tuple-element.40), channel_id=1, source_target_pairs={{0,8},{8,0},{16,24},{24,16},{1,9},{9,1},{17,25},{25,17},{2,10},{10... | collective-permute-start | bytes 2359304 | tf_op jit(solution)/shard_map/ppermute | solution.py:53
  173.1 227.6 %reduce-scatter.2.cloned.1.call-start = ((), (), s32[]{:S(2)}) async-start(), calls=%async_computation.3 | async-start | bytes 9437184 | tf_op jit(solution)/shard_map/reduce_scatter | solution.py:156
  196.3 49.2 %collective-permute-start.8 = (bf16[3072,256]{1,0:T(8,128)(2,1)S(1)}, bf16[3072,256]{1,0:T(8,128)(2,1)}, u32[]{:S(2)}, u32[]{:S(2)}) collective-permute-start(bf16[3072,256]{1,0:T(8,128)(2,1)S(1)} %maximum_select_fusion.4), channel_id=1, source_target_pairs={{8,16},{16,8},{9,17},{17,9},{10,18},{18,10},{11,19},{19,11},{12,20... | collective-permute-start | bytes 4718600 | tf_op jit(solution)/shard_map/ppermute | solution.py:53
  198.2 47.4 %collective-permute-start.7 = (bf16[3072,256]{1,0:T(8,128)(2,1)}, bf16[3072,256]{1,0:T(8,128)(2,1)S(1)}, u32[]{:S(2)}, u32[]{:S(2)}) collective-permute-start(bf16[3072,256]{1,0:T(8,128)(2,1)} %collective-permute-done.5), channel_id=1, source_target_pairs={{8,0},{16,24},{9,1},{17,25},{10,2},{18,26},{11,3},{19,27},{12,4},{... | collective-permute-start | bytes 4718600 | tf_op jit(solution)/shard_map/ppermute | solution.py:53
  245.6 38.4 %collective-permute-start.16 = (bf16[3072,256]{1,0:T(8,128)(2,1)}, bf16[3072,256]{1,0:T(8,128)(2,1)}, u32[]{:S(2)}, u32[]{:S(2)}) collective-permute-start(bf16[3072,256]{1,0:T(8,128)(2,1)} %maximum_select_fusion.5), channel_id=1, source_target_pairs={{8,16},{16,8},{9,17},{17,9},{10,18},{18,10},{11,19},{19,11},{12,20... | collective-permute-start | bytes 4718600 | tf_op jit(solution)/shard_map/ppermute | solution.py:53
  247.4 34.2 %collective-permute-start.12 = (bf16[3072,256]{1,0:T(8,128)(2,1)}, bf16[3072,256]{1,0:T(8,128)(2,1)}, u32[]{:S(2)}, u32[]{:S(2)}) collective-permute-start(bf16[3072,256]{1,0:T(8,128)(2,1)} %collective-permute-done.8), channel_id=1, source_target_pairs={{8,0},{16,24},{9,1},{17,25},{10,2},{18,26},{11,3},{19,27},{12,4},{... | collective-permute-start | bytes 4718600 | tf_op jit(solution)/shard_map/ppermute | solution.py:53
  267.8 27.7 %collective-permute-start.9 = (bf16[2048,256]{0,1:T(8,128)(2,1)S(1)}, bf16[2048,256]{0,1:T(8,128)(2,1)S(1)}, u32[]{:S(2)}, u32[]{:S(2)}) collective-permute-start(bf16[2048,256]{0,1:T(8,128)(2,1)S(1)} %broadcast_select_fusion.5), channel_id=1, source_target_pairs={{0,8},{24,16},{1,9},{25,17},{2,10},{26,18},{3,11},{27,19},{4,12},{... | collective-permute-start | bytes 3145736 | tf_op jit(solution)/shard_map/ppermute | solution.py:53
  284.0 33.1 %collective-permute-start.17 = (bf16[3072,256]{1,0:T(8,128)(2,1)}, bf16[3072,256]{1,0:T(8,128)(2,1)S(1)}, u32[]{:S(2)}, u32[]{:S(2)}) collective-permute-start(bf16[3072,256]{1,0:T(8,128)(2,1)} %collective-permute-done.16), channel_id=1, source_target_pairs={{8,0},{16,24},{9,1},{17,25},{10,2},{18,26},{11,3},{19,27},{12,4},{... | collective-permute-start | bytes 4718600 | tf_op jit(solution)/shard_map/ppermute | solution.py:53
  297.0 33.1 %collective-permute-start.10 = (bf16[2048,256]{0,1:T(8,128)(2,1)}, bf16[2048,256]{0,1:T(8,128)(2,1)}, u32[]{:S(2)}, u32[]{:S(2)}) collective-permute-start(bf16[2048,256]{0,1:T(8,128)(2,1)} %add_convert_fusion.3), channel_id=1, source_target_pairs={{8,16},{16,8},{9,17},{17,9},{10,18},{18,10},{11,19},{19,11},{12,20... | collective-permute-start | bytes 3145736 | tf_op jit(solution)/shard_map/ppermute | solution.py:53
  304.8 29.1 %collective-permute-start.13 = (bf16[2048,256]{0,1:T(8,128)(2,1)S(1)}, bf16[2048,256]{0,1:T(8,128)(2,1)S(1)}, u32[]{:S(2)}, u32[]{:S(2)}) collective-permute-start(bf16[2048,256]{0,1:T(8,128)(2,1)S(1)} %broadcast_select_fusion.4), channel_id=1, source_target_pairs={{0,8},{24,16},{1,9},{25,17},{2,10},{26,18},{3,11},{27,19},{4,12},{... | collective-permute-start | bytes 3145736 | tf_op jit(solution)/shard_map/ppermute | solution.py:53
  332.7 60.4 %collective-permute-start.11 = (bf16[1024,256]{0,1:T(8,128)(2,1)}, bf16[1024,256]{0,1:T(8,128)(2,1)}, u32[]{:S(2)}, u32[]{:S(2)}) collective-permute-start(bf16[1024,256]{0,1:T(8,128)(2,1)} %select_convert_fusion.1), channel_id=1, source_target_pairs={{0,8},{8,0},{16,24},{24,16},{1,9},{9,1},{17,25},{25,17},{2,10},{10... | collective-permute-start | bytes 1572872 | tf_op jit(solution)/shard_map/ppermute | solution.py:53
  341.9 52.6 %collective-permute-start.18 = (bf16[1024,256]{0,1:T(8,128)(2,1)}, bf16[1024,256]{0,1:T(8,128)(2,1)S(1)}, u32[]{:S(2)}, u32[]{:S(2)}) collective-permute-start(bf16[1024,256]{0,1:T(8,128)(2,1)} %get-tuple-element.94), channel_id=1, source_target_pairs={{0,8},{8,0},{16,24},{24,16},{1,9},{9,1},{17,25},{25,17},{2,10},{10... | collective-permute-start | bytes 1572872 | tf_op jit(solution)/shard_map/ppermute | solution.py:53
  365.7 28.8 %collective-permute-start.20 = (bf16[1024,256]{0,1:T(8,128)(2,1)S(1)}, bf16[1024,256]{0,1:T(8,128)(2,1)S(1)}, u32[]{:S(2)}, u32[]{:S(2)}) collective-permute-start(bf16[1024,256]{0,1:T(8,128)(2,1)S(1)} %fusion.10), channel_id=1, source_target_pairs={{0,24},{8,16},{16,8},{24,0},{1,25},{9,17},{17,9},{25,1},{2,26},{10... | collective-permute-start | bytes 1572872 | tf_op jit(solution)/shard_map/ppermute | solution.py:53
  367.6 32.7 %collective-permute-start.15 = (bf16[1024,256]{0,1:T(8,128)(2,1)S(1)}, bf16[1024,256]{0,1:T(8,128)(2,1)S(1)}, u32[]{:S(2)}, u32[]{:S(2)}) collective-permute-start(bf16[1024,256]{0,1:T(8,128)(2,1)S(1)} %select_convert_fusion), channel_id=1, source_target_pairs={{0,8},{8,0},{16,24},{24,16},{1,9},{9,1},{17,25},{25,17},{2,10},{10... | collective-permute-start | bytes 1572872 | tf_op jit(solution)/shard_map/ppermute | solution.py:53
  430.9 28.3 %collective-permute-start.27 = (bf16[256,1536]{1,0:T(8,128)(2,1)S(1)}, bf16[256,1536]{1,0:T(8,128)(2,1)S(1)}, u32[]{:S(2)}, u32[]{:S(2)}) collective-permute-start(bf16[256,1536]{1,0:T(8,128)(2,1)S(1)} %pad_maximum_fusion.5), channel_id=1, source_target_pairs={{0,2},{1,3},{2,0},{3,1},{4,6},{5,7},{6,4},{7,5},{8,10},{9,11},{10,... | collective-permute-start | bytes 2359304 | tf_op jit(solution)/shard_map/ppermute | solution.py:93
  431.4 29.7 %collective-permute-start.24 = (bf16[256,1536]{1,0:T(8,128)(2,1)S(1)}, bf16[256,1536]{1,0:T(8,128)(2,1)S(1)}, u32[]{:S(2)}, u32[]{:S(2)}) collective-permute-start(bf16[256,1536]{1,0:T(8,128)(2,1)S(1)} %concatenate.89), channel_id=1, source_target_pairs={{0,4},{1,5},{2,6},{3,7},{4,0},{5,1},{6,2},{7,3},{8,12},{9,13},{10,... | collective-permute-start | bytes 2359304 | tf_op jit(solution)/shard_map/ppermute | solution.py:93
  433.2 46.0 %collective-permute-start.29 = (bf16[256,1536]{1,0:T(8,128)(2,1)S(1)}, bf16[256,1536]{1,0:T(8,128)(2,1)S(1)}, u32[]{:S(2)}, u32[]{:S(2)}) collective-permute-start(bf16[256,1536]{1,0:T(8,128)(2,1)S(1)} %concatenate.90), channel_id=1, source_target_pairs={{0,4},{1,5},{2,6},{3,7},{4,0},{5,1},{6,2},{7,3},{8,12},{9,13},{10,... | collective-permute-start | bytes 2359304 | tf_op jit(solution)/shard_map/ppermute | solution.py:93
  443.1 34.1 %collective-permute-start.23 = (bf16[256,768]{1,0:T(8,128)(2,1)S(1)}, bf16[256,768]{1,0:T(8,128)(2,1)S(1)}, u32[]{:S(2)}, u32[]{:S(2)}) collective-permute-start(bf16[256,768]{1,0:T(8,128)(2,1)S(1)} %add_convert_fusion.13), channel_id=1, source_target_pairs={{0,4},{1,5},{2,6},{3,7},{4,0},{5,1},{6,2},{7,3},{8,12},{9,13},{10,... | collective-permute-start | bytes 1179656 | tf_op jit(solution)/shard_map/ppermute | solution.py:93
  459.3 25.0 %collective-permute-start.28 = (bf16[256,768]{1,0:T(8,128)(2,1)S(1)}, bf16[256,768]{1,0:T(8,128)(2,1)S(1)}, u32[]{:S(2)}, u32[]{:S(2)}) collective-permute-start(bf16[256,768]{1,0:T(8,128)(2,1)S(1)} %add_convert_fusion.9), channel_id=1, source_target_pairs={{0,4},{1,5},{2,6},{3,7},{4,0},{5,1},{6,2},{7,3},{8,12},{9,13},{10,... | collective-permute-start | bytes 1179656 | tf_op jit(solution)/shard_map/ppermute | solution.py:93
  (19 other events, 377.3 us)
Sparse Core Ops, SparseCore 0:
  9.9 57.0 all-gather.2
  173.2 71.7 all-gather.4
  251.7 74.3 reduce-scatter.1

commit v5 on v4

--- a/solution.py
+++ b/solution.py
@@ -96,16 +96,19 @@
     kept = []
     cuts = 2
     size = rows.shape[0] // cuts
+    parts = [rows[s * size : (s + 1) * size] for s in range(cuts)]
+    away = [contract_last(part, right_rel[4 * width :]).astype(rows.dtype) for part in parts]
+    here = [contract_last(part, right_rel[: 4 * width]).astype(rows.dtype) for part in parts]
+    here = together(here, *away)
     for s in range(cuts):
-        part = rows[s * size : (s + 1) * size]
-        part = after(part, mine) if s else part
-        away = contract_last(part, right_rel[4 * width :]).astype(rows.dtype)
-        here = contract_last(part, right_rel[: 4 * width]).astype(rows.dtype)
-        mine = add(after(here, away), swap(away, 1))
+        mine = add(here[s], swap(away[s], 1))
         half = size // 2
         block = lambda b, h: mine[h * half : (h + 1) * half, b * width : (b + 1) * width]
-        by_x = swap(jnp.concatenate([block(1, 0), block(3, 0)], axis=1), 2)
-        by_y = swap(jnp.concatenate([block(2, 1), block(3, 1)], axis=1), 4)
+        to_x = jnp.concatenate([block(1, 0), block(3, 0)], axis=1)
+        to_y = jnp.concatenate([block(2, 1), block(3, 1)], axis=1)
+        to_x, to_y = together([to_x, to_y])
+        by_x = swap(to_x, 2)
+        by_y = swap(to_y, 4)
         then_y = swap(add(block(2, 0), by_x[:, width:]), 4)
         then_x = swap(add(block(1, 1), by_y[:, width:]), 2)
         kept.append(block(0, 0).astype(F32) + by_x[:, :width].astype(F32) + then_y.astype(F32))
@@ -132,26 +135,29 @@
 
     mirror = send(gradient, MIRROR)
     pair = send(gradient, PAIRS)
+    columns = line.placed(jnp.zeros((4 * height, width), BF16), gradient, 0)
 
     relay, own0 = together([jnp.where(line.inner, mirror, gradient), own0], pair)
     relay = send(relay, RELAY)
     pair0 = send(own0, PAIRS)
-    columns = jnp.zeros((4 * height, width), BF16)
-    for bits, piece in ((0, gradient), (1, pair), (3, mirror)):
-        columns = line.placed(columns, piece, bits)
-
-    near0, own1, own2 = together([line.near(own0, pair0), own1, own2], relay)
+    turn = lambda x, bits: contract_first(line.block(left_cols, bits), x)
+    left_sum = turn(gradient, 0) + turn(pair, 1) + turn(mirror, 3)
+
+    near0, own1 = together([line.near(own0, pair0), own1], left_sum)
     middle0 = send(near0, MIDDLE)
     pair1 = send(own1, PAIRS)
-    pair2 = send(own2, PAIRS)
-    columns = line.placed(columns, after(relay, pair1), 2)
-    left_part = contract_first(left_cols, columns).astype(BF16)
+    near1 = line.near(own1, pair1)
+
+    left_part = (left_sum + turn(after(relay, near1, middle0), 2)).astype(BF16)
     left_rotated = lax.all_gather(left_part, "col", axis=1, tiled=True)
 
-    middle0, near1 = together([middle0, line.near(own1, pair1)], pair2, left_part)
+    middle0, near1, own2 = together([middle0, near1, own2])
     out0 = send(middle0, OUTWARD)
     middle1 = send(near1, MIDDLE)
-    product = contract_last(after(columns, near1), gradient).astype(BF16)
+    pair2 = send(own2, PAIRS)
+    for bits, piece in zip((1, 3, 2), together([pair, mirror, relay], left_part)):
+        columns = line.placed(columns, piece, bits)
+    product = contract_last(columns, gradient).astype(BF16)
     product = after(product, left_rotated)
     product = lax.psum_scatter(product, "col", scatter_dimension=0, tiled=True).astype(F32)
     left_next = 0.95 * left_stat + 0.05 * product

time: 510 us -> 515 us (level)
  waiting for transfers between devices: 247 us -> 218 us
  starting transfers between devices: 83.6 us -> 111 us
    ppermute x21, waiting for transfers between devices: 193 us -> 152 us  [send(): return lax.ppermute(x, self.axis, pairs)]
    ppermute x21, starting transfers between devices: 71.9 us -> 98.7 us  [send(): return lax.ppermute(x, self.axis, pairs)]
    all_gather x1, waiting for transfers between devices: 0.02 us -> 12.2 us  [body_on_line(): left_rotated = lax.all_gather(left_part, 'col', axis=1, tiled=True)]
    dot_general x1 -> x4, matrix products: 12.1 us -> 17.3 us  [contract_first(): lax.dot_general(first, second, (((0,), (0,)), ((), ())), preferred_elemen...]
  transfers between devices with their start and end apart: 34 -> 34, of which waited for: 16 -> 15; matrix products, arithmetic and copies ran while one was open for 25% -> 29% of each run, Pallas kernels for 0% -> 0%
where the time goes in v5:
time: 515 us; the launch traced here: 506 us
  waiting for transfers between devices  218 us (42%)
  starting transfers between devices  111 us (22%)
  matrix products  98.3 us (19%)
  other arithmetic  39.3 us (8%)
  local copies, waits for them, and re-layouts  25.4 us (5%)
  between operations  14.7 us (3%)
    ppermute x21, waiting for transfers between devices, send(): return lax.ppermute(x, self.axis, pairs)  152 us
    ppermute x21, starting transfers between devices, send(): return lax.ppermute(x, self.axis, pairs)  98.7 us
    ppermute x10, waiting for transfers between devices, swap(): return lax.ppermute(x, axis, [(j, j ^ bit) for j in range(8)])  53 us
    dot_general x5, matrix products, contract_last(): lax.dot_general(first, second, (((1,), (1,)), ((), ())), preferred_elemen...  33.2 us
    dot_general x3, matrix products, part(): rotated = jnp.dot(left_rotated, right_part, preferred_element_type=F32)  29 us
    dot_general x3, matrix products, part(): jnp.dot(left_cols, after(normalized, *earlier), preferred_element_type=F32)  18.7 us
    dot_general x4, matrix products, contract_first(): lax.dot_general(first, second, (((0,), (0,)), ((), ())), preferred_elemen...  17.3 us
    all_gather x1, waiting for transfers between devices, body_on_line(): left_rotated = lax.all_gather(left_part, 'col', axis=1, tiled=True)  12.2 us
  transfers between devices with their start and end apart: 34, of which 15 were waited for; matrix products, arithmetic and copies ran while one was open for 29% of the time, Pallas kernels for 0%

profile of v5, /device:TPU:0, one launch (start us, length us, event | category | flops | bytes accessed | tf_op | source)
XLA Modules:
  0.0 506.3 jit_solution(12274219662206022614)
XLA Ops:
  16.0 32.6 %collective-permute-done.1 = bf16[1024,768]{1,0:T(8,128)(2,1)S(1)} collective-permute-done((bf16[1024,768]{1,0:T(8,128)(2,1)}, bf16[1024,768]{1,0:T(8,128)(2,1)S(1)}, u32[]{:S(2)}, u32[]{:S(2)}) %collective-permute-start.1) | collective-permute-done | bytes 1572896 | tf_op jit(solution)/shard_map/ppermute | solution.py:53
  53.9 27.7 %collective-permute-done = bf16[1024,768]{1,0:T(8,128)(2,1)} collective-permute-done((bf16[1024,768]{1,0:T(8,128)(2,1)}, bf16[1024,768]{1,0:T(8,128)(2,1)}, u32[]{:S(2)}, u32[]{:S(2)}) %collective-permute-start) | collective-permute-done | bytes 1572896 | tf_op jit(solution)/shard_map/ppermute | solution.py:53
  87.5 17.5 %collective-permute-done.3 = bf16[1536,256]{1,0:T(8,128)(2,1)} collective-permute-done((bf16[1536,256]{1,0:T(8,128)(2,1)S(1)}, bf16[1536,256]{1,0:T(8,128)(2,1)}, u32[]{:S(2)}, u32[]{:S(2)}) %collective-permute-start.3) | collective-permute-done | bytes 786464 | tf_op jit(solution)/shard_map/ppermute | solution.py:53
  125.0 29.0 %collective-permute-done.4 = bf16[1536,256]{1,0:T(8,128)(2,1)} collective-permute-done((bf16[1536,256]{1,0:T(8,128)(2,1)}, bf16[1536,256]{1,0:T(8,128)(2,1)}, u32[]{:S(2)}, u32[]{:S(2)}) %collective-permute-start.4) | collective-permute-done | bytes 786464 | tf_op jit(solution)/shard_map/ppermute | solution.py:53
  156.5 5.7 %add_convert_fusion.2 = bf16[1024,768]{1,0:T(8,128)(2,1)} fusion(f32[1024,768]{1,0:T(8,128)S(1)} %copy-done.16, bf16[1024,768]{1,0:T(8,128)(2,1)} %collective-permute-done.2, bf16[4096,1024]{1,0:T(8,128)(2,1)} %all-gather.3.cloned.1.call-done, s32[]{:T(128)S(6)} %select_n.165), kind=kOutput, calls=%fused_computation.21 | convolution fusion | flops 1612185600 | bytes 8388612 | tf_op jit(solution)/shard_map/dot_general | solution.py:24
  162.3 16.5 %collective-permute-start.8 = (bf16[1536,256]{1,0:T(8,128)(2,1)}, bf16[1536,256]{1,0:T(8,128)(2,1)}, u32[]{:S(2)}, u32[]{:S(2)}) collective-permute-start(bf16[1536,256]{1,0:T(8,128)(2,1)} %get-tuple-element.51), channel_id=1, source_target_pairs={{0,8},{8,0},{16,24},{24,16},{1,9},{9,1},{17,25},{25,17},{2,10},{10... | collective-permute-start | bytes 2359304 | tf_op jit(solution)/shard_map/ppermute | solution.py:53
  189.1 11.9 %convolution_convert_fusion = bf16[4096,1024]{1,0:T(8,128)(2,1)} fusion(bf16[4096,768]{1,0:T(8,128)(2,1)} %constant_dynamic-update-slice_fusion.3, bf16[1024,768]{1,0:T(8,128)(2,1)S(1)} %copy-done.11), kind=kOutput, calls=%fused_computation | convolution fusion | flops 6446645248 | bytes 16252928 | tf_op jit(solution)/shard_map/dot_general | solution.py:20
  203.9 26.6 %collective-permute-done.6 = bf16[3072,256]{1,0:T(8,128)(2,1)} collective-permute-done((bf16[3072,256]{1,0:T(8,128)(2,1)}, bf16[3072,256]{1,0:T(8,128)(2,1)}, u32[]{:S(2)}, u32[]{:S(2)}) %collective-permute-start.6) | collective-permute-done | bytes 1572896 | tf_op jit(solution)/shard_map/ppermute | solution.py:53
  236.1 12.2 %all-gather.5.cloned.1.call-done = bf16[1024,6144]{1,0:T(8,128)(2,1)} async-done(((bf16[1024,768]{1,0:T(8,128)(2,1)}), bf16[1024,6144]{1,0:T(8,128)(2,1)}) %all-gather.5.cloned.1.call-update) | async-done | bytes 12582928 | tf_op jit(solution)/shard_map/all_gather | solution.py:152
  248.3 9.1 %divide_convert_fusion.2 = (bf16[1024,256]{1,0:T(8,128)(2,1)S(1)}, f32[1024,256]{1,0:T(8,128)S(1)}, f32[1024,256]{1,0:T(8,128)S(1)}) fusion(f32[1024,768]{1,0:T(8,128)} %param.10, f32[1024,768]{1,0:T(8,128)} %param.11, bf16[1024,6144]{1,0:T(8,128)(2,1)} %all-gather.5.cloned.1.call-done, bf16[6144,256]{1,0:T(8,128)(2,1)S(1)} %maximum_select_fusion), kind=kOutput, calls=%fused_computation.73 | convolution fusion | flops 3224371200 | bytes 20447232 | tf_op jit(solution)/shard_map/dot_general | solution.py:172
  257.5 6.8 %fusion = bf16[4096,256]{0,1:T(8,128)(2,1)S(1)} fusion(bf16[1024,256]{1,0:T(8,128)(2,1)S(1)} %get-tuple-element.90, bf16[4096,1024]{1,0:T(8,128)(2,1)} %all-gather.3.cloned.1.call-done), kind=kOutput, calls=%fused_computation.6 | convolution fusion | flops 2148532224 | bytes 11010048 | tf_op jit(solution)/shard_map/dot_general | solution.py:176
  272.8 14.4 %collective-permute-start.17 = (bf16[3072,256]{1,0:T(8,128)(2,1)}, bf16[3072,256]{1,0:T(8,128)(2,1)S(1)}, u32[]{:S(2)}, u32[]{:S(2)}) collective-permute-start(bf16[3072,256]{1,0:T(8,128)(2,1)} %collective-permute-done.16), channel_id=1, source_target_pairs={{8,0},{16,24},{9,1},{17,25},{10,2},{18,26},{11,3},{19,27},{12,4},{... | collective-permute-start | bytes 4718600 | tf_op jit(solution)/shard_map/ppermute | solution.py:53
  287.2 9.7 %divide_convert_fusion.1 = (bf16[1024,256]{1,0:T(8,128)(2,1)S(1)}, f32[1024,256]{1,0:T(8,128)S(1)}, f32[1024,256]{1,0:T(8,128)S(1)}) fusion(f32[1024,768]{1,0:T(8,128)} %param.10, f32[1024,768]{1,0:T(8,128)} %param.11, bf16[1024,6144]{1,0:T(8,128)(2,1)} %all-gather.5.cloned.1.call-done, bf16[6144,256]{1,0:T(8,128)(2,1)S(1)} %maximum_select_fusion.1), kind=kOutput, calls=%fused_computation.69 | convolution fusion | flops 3224371200 | bytes 20447232 | tf_op jit(solution)/shard_map/dot_general | solution.py:172
  300.1 6.0 %fusion.1 = bf16[4096,256]{0,1:T(8,128)(2,1)S(1)} fusion(bf16[1024,256]{1,0:T(8,128)(2,1)S(1)} %get-tuple-element.56, bf16[4096,1024]{1,0:T(8,128)(2,1)} %all-gather.3.cloned.1.call-done), kind=kOutput, calls=%fused_computation.7 | convolution fusion | flops 2148532224 | bytes 11010048 | tf_op jit(solution)/shard_map/dot_general | solution.py:176
  306.1 5.7 %collective-permute-start.13 = (bf16[2048,256]{0,1:T(8,128)(2,1)S(1)}, bf16[2048,256]{0,1:T(8,128)(2,1)S(1)}, u32[]{:S(2)}, u32[]{:S(2)}) collective-permute-start(bf16[2048,256]{0,1:T(8,128)(2,1)S(1)} %broadcast_select_fusion.4), channel_id=1, source_target_pairs={{0,8},{24,16},{1,9},{25,17},{2,10},{26,18},{3,11},{27,19},{4,12},{... | collective-permute-start | bytes 3145736 | tf_op jit(solution)/shard_map/ppermute | solution.py:53
  314.4 10.2 %divide_convert_fusion = (bf16[1024,256]{1,0:T(8,128)(2,1)S(1)}, f32[1024,256]{1,0:T(8,128)S(1)}, f32[1024,256]{1,0:T(8,128)}) fusion(f32[1024,768]{1,0:T(8,128)} %param.10, f32[1024,768]{1,0:T(8,128)} %param.11, bf16[1024,6144]{1,0:T(8,128)(2,1)} %all-gather.5.cloned.1.call-done, bf16[6144,256]{1,0:T(8,128)(2,1)S(1)} %maximum_select_fusion.2), kind=kOutput, calls=%fused_computation.65 | convolution fusion | flops 3224371200 | bytes 20447232 | tf_op jit(solution)/shard_map/dot_general | solution.py:172
  329.4 5.9 %collective-permute-done.13 = bf16[2048,256]{0,1:T(8,128)(2,1)S(1)} collective-permute-done((bf16[2048,256]{0,1:T(8,128)(2,1)S(1)}, bf16[2048,256]{0,1:T(8,128)(2,1)S(1)}, u32[]{:S(2)}, u32[]{:S(2)}) %collective-permute-start.13) | collective-permute-done | bytes 1048608 | tf_op jit(solution)/shard_map/ppermute | solution.py:53
  336.3 6.0 %convolution_convert_fusion.1 = bf16[256,4096]{1,0:T(8,128)(2,1)S(1)} fusion(bf16[1024,256]{1,0:T(8,128)(2,1)S(1)} %get-tuple-element.59, bf16[4096,1024]{1,0:T(8,128)(2,1)} %all-gather.3.cloned.1.call-done), kind=kOutput, calls=%fused_computation.3 | convolution fusion | flops 2148532224 | bytes 11010048 | tf_op jit(solution)/shard_map/dot_general | solution.py:176
  372.4 23.6 %collective-permute-start.15 = (bf16[1024,256]{0,1:T(8,128)(2,1)S(1)}, bf16[1024,256]{0,1:T(8,128)(2,1)S(1)}, u32[]{:S(2)}, u32[]{:S(2)}) collective-permute-start(bf16[1024,256]{0,1:T(8,128)(2,1)S(1)} %select_convert_fusion), channel_id=1, source_target_pairs={{0,8},{8,0},{16,24},{24,16},{1,9},{9,1},{17,25},{25,17},{2,10},{10... | collective-permute-start | bytes 1572872 | tf_op jit(solution)/shard_map/ppermute | solution.py:53
  407.8 5.5 %convolution_convert_fusion.4 = bf16[512,3072]{1,0:T(8,128)(2,1)S(1)} fusion(bf16[6144,768]{1,0:T(8,128)(2,1)} %dynamic-slice_dynamic-update-slice_fusion, bf16[1024,768]{0,1:T(8,128)(2,1)S(1)} %copy-done.9), kind=kOutput, calls=%fused_computation.8 | convolution fusion | flops 2417491968 | bytes 8650752 | tf_op jit(solution)/shard_map/dot_general | solution.py:20
  436.8 14.9 %collective-permute-done.27 = bf16[256,1536]{1,0:T(8,128)(2,1)S(1)} collective-permute-done((bf16[256,1536]{1,0:T(8,128)(2,1)S(1)}, bf16[256,1536]{1,0:T(8,128)(2,1)S(1)}, u32[]{:S(2)}, u32[]{:S(2)}) %collective-permute-start.27) | collective-permute-done | bytes 786464 | tf_op jit(solution)/shard_map/ppermute | solution.py:93
  453.5 14.1 %collective-permute-done.22 = bf16[256,1536]{1,0:T(8,128)(2,1)S(1)} collective-permute-done((bf16[256,1536]{1,0:T(8,128)(2,1)S(1)}, bf16[256,1536]{1,0:T(8,128)(2,1)S(1)}, u32[]{:S(2)}, u32[]{:S(2)}) %collective-permute-start.22) | collective-permute-done | bytes 786464 | tf_op jit(solution)/shard_map/ppermute | solution.py:93
  469.8 10.7 %collective-permute-done.28 = bf16[256,768]{1,0:T(8,128)(2,1)S(1)} collective-permute-done((bf16[256,768]{1,0:T(8,128)(2,1)S(1)}, bf16[256,768]{1,0:T(8,128)(2,1)S(1)}, u32[]{:S(2)}, u32[]{:S(2)}) %collective-permute-start.28) | collective-permute-done | bytes 393248 | tf_op jit(solution)/shard_map/ppermute | solution.py:93
  489.9 8.1 %collective-permute-done.25 = bf16[256,768]{1,0:T(8,128)(2,1)S(1)} collective-permute-done((bf16[256,768]{1,0:T(8,128)(2,1)S(1)}, bf16[256,768]{1,0:T(8,128)(2,1)S(1)}, u32[]{:S(2)}, u32[]{:S(2)}) %collective-permute-start.25) | collective-permute-done | bytes 393248 | tf_op jit(solution)/shard_map/ppermute | solution.py:93
  (153 shorter events, 161.4 us)
Async XLA Ops:
  7.2 100.1 %all-gather.3.cloned.1.call-start = ((), (), s32[]{:S(2)}) async-start(), calls=%async_computation.1 | async-start | bytes 9437184 | tf_op jit(solution)/shard_map/all_gather | solution.py:133
  7.9 240.4 %all-gather.5.cloned.1.call-start = ((), (), s32[]{:S(2)}) async-start(), calls=%async_computation.2 | async-start | bytes 14155776 | tf_op jit(solution)/shard_map/all_gather | solution.py:152
  7.9 40.6 %collective-permute-start.1 = (bf16[1024,768]{1,0:T(8,128)(2,1)}, bf16[1024,768]{1,0:T(8,128)(2,1)S(1)}, u32[]{:S(2)}, u32[]{:S(2)}) collective-permute-start(bf16[1024,768]{1,0:T(8,128)(2,1)} %param.6), channel_id=1, source_target_pairs={{0,24},{8,16},{16,8},{24,0},{1,25},{9,17},{17,9},{25,1},{2,26},{10... | collective-permute-start | bytes 4718600 | tf_op jit(solution)/shard_map/ppermute | solution.py:53
  13.1 68.5 %collective-permute-start = (bf16[1024,768]{1,0:T(8,128)(2,1)}, bf16[1024,768]{1,0:T(8,128)(2,1)}, u32[]{:S(2)}, u32[]{:S(2)}) collective-permute-start(bf16[1024,768]{1,0:T(8,128)(2,1)} %param.6), channel_id=1, source_target_pairs={{0,8},{8,0},{16,24},{24,16},{1,9},{9,1},{17,25},{25,17},{2,10},{10... | collective-permute-start | bytes 4718600 | tf_op jit(solution)/shard_map/ppermute | solution.py:53
  86.4 70.1 %collective-permute-start.2 = (bf16[1024,768]{1,0:T(8,128)(2,1)}, bf16[1024,768]{1,0:T(8,128)(2,1)}, u32[]{:S(2)}, u32[]{:S(2)}) collective-permute-start(bf16[1024,768]{1,0:T(8,128)(2,1)} %get-tuple-element.44), channel_id=1, source_target_pairs={{0,16},{8,0},{16,24},{24,8},{1,17},{9,1},{17,25},{25,9},{2,18},{10... | collective-permute-start | bytes 4718600 | tf_op jit(solution)/shard_map/ppermute | solution.py:53
  119.5 37.0 %collective-permute-start.5 = (bf16[3072,256]{1,0:T(8,128)(2,1)S(1)}, bf16[3072,256]{1,0:T(8,128)(2,1)}, u32[]{:S(2)}, u32[]{:S(2)}) collective-permute-start(bf16[3072,256]{1,0:T(8,128)(2,1)S(1)} %maximum_select_fusion.3), channel_id=1, source_target_pairs={{8,16},{16,8},{9,17},{17,9},{10,18},{18,10},{11,19},{19,11},{12,20... | collective-permute-start | bytes 4718600 | tf_op jit(solution)/shard_map/ppermute | solution.py:53
  121.3 32.7 %collective-permute-start.4 = (bf16[1536,256]{1,0:T(8,128)(2,1)}, bf16[1536,256]{1,0:T(8,128)(2,1)}, u32[]{:S(2)}, u32[]{:S(2)}) collective-permute-start(bf16[1536,256]{1,0:T(8,128)(2,1)} %get-tuple-element.46), channel_id=1, source_target_pairs={{0,8},{8,0},{16,24},{24,16},{1,9},{9,1},{17,25},{25,17},{2,10},{10... | collective-permute-start | bytes 2359304 | tf_op jit(solution)/shard_map/ppermute | solution.py:53
  162.2 242.6 %reduce-scatter.2.cloned.1.call-start = ((), (), s32[]{:S(2)}) async-start(), calls=%async_computation.3 | async-start | bytes 9437184 | tf_op jit(solution)/shard_map/reduce_scatter | solution.py:162
  162.3 38.7 %collective-permute-start.8 = (bf16[1536,256]{1,0:T(8,128)(2,1)}, bf16[1536,256]{1,0:T(8,128)(2,1)}, u32[]{:S(2)}, u32[]{:S(2)}) collective-permute-start(bf16[1536,256]{1,0:T(8,128)(2,1)} %get-tuple-element.51), channel_id=1, source_target_pairs={{0,8},{8,0},{16,24},{24,16},{1,9},{9,1},{17,25},{25,17},{2,10},{10... | collective-permute-start | bytes 2359304 | tf_op jit(solution)/shard_map/ppermute | solution.py:53
  178.8 51.8 %collective-permute-start.6 = (bf16[3072,256]{1,0:T(8,128)(2,1)}, bf16[3072,256]{1,0:T(8,128)(2,1)}, u32[]{:S(2)}, u32[]{:S(2)}) collective-permute-start(bf16[3072,256]{1,0:T(8,128)(2,1)} %collective-permute-done.5), channel_id=1, source_target_pairs={{8,0},{16,24},{9,1},{17,25},{10,2},{18,26},{11,3},{19,27},{12,4},{... | collective-permute-start | bytes 4718600 | tf_op jit(solution)/shard_map/ppermute | solution.py:53
  180.1 50.5 %collective-permute-start.7 = (bf16[3072,256]{1,0:T(8,128)(2,1)S(1)}, bf16[3072,256]{1,0:T(8,128)(2,1)}, u32[]{:S(2)}, u32[]{:S(2)}) collective-permute-start(bf16[3072,256]{1,0:T(8,128)(2,1)S(1)} %maximum_select_fusion.4), channel_id=1, source_target_pairs={{8,16},{16,8},{9,17},{17,9},{10,18},{18,10},{11,19},{19,11},{12,20... | collective-permute-start | bytes 4718600 | tf_op jit(solution)/shard_map/ppermute | solution.py:53
  230.5 42.3 %collective-permute-start.16 = (bf16[3072,256]{1,0:T(8,128)(2,1)}, bf16[3072,256]{1,0:T(8,128)(2,1)}, u32[]{:S(2)}, u32[]{:S(2)}) collective-permute-start(bf16[3072,256]{1,0:T(8,128)(2,1)} %maximum_select_fusion.5), channel_id=1, source_target_pairs={{8,16},{16,8},{9,17},{17,9},{10,18},{18,10},{11,19},{19,11},{12,20... | collective-permute-start | bytes 4718600 | tf_op jit(solution)/shard_map/ppermute | solution.py:53
  232.3 38.0 %collective-permute-start.12 = (bf16[3072,256]{1,0:T(8,128)(2,1)}, bf16[3072,256]{1,0:T(8,128)(2,1)}, u32[]{:S(2)}, u32[]{:S(2)}) collective-permute-start(bf16[3072,256]{1,0:T(8,128)(2,1)} %collective-permute-done.7), channel_id=1, source_target_pairs={{8,0},{16,24},{9,1},{17,25},{10,2},{18,26},{11,3},{19,27},{12,4},{... | collective-permute-start | bytes 4718600 | tf_op jit(solution)/shard_map/ppermute | solution.py:53
  264.4 32.5 %collective-permute-start.9 = (bf16[2048,256]{0,1:T(8,128)(2,1)S(1)}, bf16[2048,256]{0,1:T(8,128)(2,1)S(1)}, u32[]{:S(2)}, u32[]{:S(2)}) collective-permute-start(bf16[2048,256]{0,1:T(8,128)(2,1)S(1)} %broadcast_select_fusion.5), channel_id=1, source_target_pairs={{0,8},{24,16},{1,9},{25,17},{2,10},{26,18},{3,11},{27,19},{4,12},{... | collective-permute-start | bytes 3145736 | tf_op jit(solution)/shard_map/ppermute | solution.py:53
  272.8 39.0 %collective-permute-start.17 = (bf16[3072,256]{1,0:T(8,128)(2,1)}, bf16[3072,256]{1,0:T(8,128)(2,1)S(1)}, u32[]{:S(2)}, u32[]{:S(2)}) collective-permute-start(bf16[3072,256]{1,0:T(8,128)(2,1)} %collective-permute-done.16), channel_id=1, source_target_pairs={{8,0},{16,24},{9,1},{17,25},{10,2},{18,26},{11,3},{19,27},{12,4},{... | collective-permute-start | bytes 4718600 | tf_op jit(solution)/shard_map/ppermute | solution.py:53
  306.1 29.2 %collective-permute-start.13 = (bf16[2048,256]{0,1:T(8,128)(2,1)S(1)}, bf16[2048,256]{0,1:T(8,128)(2,1)S(1)}, u32[]{:S(2)}, u32[]{:S(2)}) collective-permute-start(bf16[2048,256]{0,1:T(8,128)(2,1)S(1)} %broadcast_select_fusion.4), channel_id=1, source_target_pairs={{0,8},{24,16},{1,9},{25,17},{2,10},{26,18},{3,11},{27,19},{4,12},{... | collective-permute-start | bytes 3145736 | tf_op jit(solution)/shard_map/ppermute | solution.py:53
  327.3 68.7 %collective-permute-start.11 = (bf16[1024,256]{0,1:T(8,128)(2,1)}, bf16[1024,256]{0,1:T(8,128)(2,1)}, u32[]{:S(2)}, u32[]{:S(2)}) collective-permute-start(bf16[1024,256]{0,1:T(8,128)(2,1)} %select_convert_fusion.1), channel_id=1, source_target_pairs={{0,8},{8,0},{16,24},{24,16},{1,9},{9,1},{17,25},{25,17},{2,10},{10... | collective-permute-start | bytes 1572872 | tf_op jit(solution)/shard_map/ppermute | solution.py:53
  343.4 54.0 %collective-permute-start.18 = (bf16[1024,256]{0,1:T(8,128)(2,1)}, bf16[1024,256]{0,1:T(8,128)(2,1)S(1)}, u32[]{:S(2)}, u32[]{:S(2)}) collective-permute-start(bf16[1024,256]{0,1:T(8,128)(2,1)} %get-tuple-element.104), channel_id=1, source_target_pairs={{0,8},{8,0},{16,24},{24,16},{1,9},{9,1},{17,25},{25,17},{2,10},{10... | collective-permute-start | bytes 1572872 | tf_op jit(solution)/shard_map/ppermute | solution.py:53
  366.5 31.0 %collective-permute-start.20 = (bf16[1024,256]{0,1:T(8,128)(2,1)S(1)}, bf16[1024,256]{0,1:T(8,128)(2,1)S(1)}, u32[]{:S(2)}, u32[]{:S(2)}) collective-permute-start(bf16[1024,256]{0,1:T(8,128)(2,1)S(1)} %fusion.21), channel_id=1, source_target_pairs={{0,24},{8,16},{16,8},{24,0},{1,25},{9,17},{17,9},{25,1},{2,26},{10... | collective-permute-start | bytes 1572872 | tf_op jit(solution)/shard_map/ppermute | solution.py:53
  372.4 30.8 %collective-permute-start.15 = (bf16[1024,256]{0,1:T(8,128)(2,1)S(1)}, bf16[1024,256]{0,1:T(8,128)(2,1)S(1)}, u32[]{:S(2)}, u32[]{:S(2)}) collective-permute-start(bf16[1024,256]{0,1:T(8,128)(2,1)S(1)} %select_convert_fusion), channel_id=1, source_target_pairs={{0,8},{8,0},{16,24},{24,16},{1,9},{9,1},{17,25},{25,17},{2,10},{10... | collective-permute-start | bytes 1572872 | tf_op jit(solution)/shard_map/ppermute | solution.py:53
  434.2 33.4 %collective-permute-start.22 = (bf16[256,1536]{1,0:T(8,128)(2,1)S(1)}, bf16[256,1536]{1,0:T(8,128)(2,1)S(1)}, u32[]{:S(2)}, u32[]{:S(2)}) collective-permute-start(bf16[256,1536]{1,0:T(8,128)(2,1)S(1)} %pad_maximum_fusion.4), channel_id=1, source_target_pairs={{0,2},{1,3},{2,0},{3,1},{4,6},{5,7},{6,4},{7,5},{8,10},{9,11},{10,... | collective-permute-start | bytes 2359304 | tf_op jit(solution)/shard_map/ppermute | solution.py:93
  434.7 35.0 %collective-permute-start.29 = (bf16[256,1536]{1,0:T(8,128)(2,1)S(1)}, bf16[256,1536]{1,0:T(8,128)(2,1)S(1)}, u32[]{:S(2)}, u32[]{:S(2)}) collective-permute-start(bf16[256,1536]{1,0:T(8,128)(2,1)S(1)} %concatenate.90), channel_id=1, source_target_pairs={{0,4},{1,5},{2,6},{3,7},{4,0},{5,1},{6,2},{7,3},{8,12},{9,13},{10,... | collective-permute-start | bytes 2359304 | tf_op jit(solution)/shard_map/ppermute | solution.py:93
  436.6 46.0 %collective-permute-start.24 = (bf16[256,1536]{1,0:T(8,128)(2,1)S(1)}, bf16[256,1536]{1,0:T(8,128)(2,1)S(1)}, u32[]{:S(2)}, u32[]{:S(2)}) collective-permute-start(bf16[256,1536]{1,0:T(8,128)(2,1)S(1)} %concatenate.89), channel_id=1, source_target_pairs={{0,4},{1,5},{2,6},{3,7},{4,0},{5,1},{6,2},{7,3},{8,12},{9,13},{10,... | collective-permute-start | bytes 2359304 | tf_op jit(solution)/shard_map/ppermute | solution.py:93
  451.8 28.7 %collective-permute-start.28 = (bf16[256,768]{1,0:T(8,128)(2,1)S(1)}, bf16[256,768]{1,0:T(8,128)(2,1)S(1)}, u32[]{:S(2)}, u32[]{:S(2)}) collective-permute-start(bf16[256,768]{1,0:T(8,128)(2,1)S(1)} %add_convert_fusion.10), channel_id=1, source_target_pairs={{0,4},{1,5},{2,6},{3,7},{4,0},{5,1},{6,2},{7,3},{8,12},{9,13},{10,... | collective-permute-start | bytes 1179656 | tf_op jit(solution)/shard_map/ppermute | solution.py:93
  (27 other events, 525.7 us)
Sparse Core Ops, SparseCore 0:
  9.9 57.0 all-gather.2
  162.3 85.9 all-gather.4
  251.8 71.2 reduce-scatter.1
